TPU v7x, 32 devices: a whole 2x2x4 slice. The times are simulated.
32 devices in a mesh: group: 4 (over y, x), inner: 8 (over z, core).
Axes of the slice: x: 2, y: 2, z: 4, core: 2. Of those that a mesh axis runs over, the one named last changes fastest.
Arguments:
- tokens: bfloat16 [1024, 2048], P(('group', 'inner')), may hold values from -6 to 6
- upstream: bfloat16 [1024, 2048], P(('group', 'inner')), may hold values from -6 to 6
- gate_weights: float32 [1024, 8], P(('group', 'inner')), may hold values from 0.05 to 0.5
- group_choice: int32 [1024, 4], P(('group', 'inner')), may hold values from 0 to 7, all different within a row
- pair_pick: int32 [1024, 4, 2], P(('group', 'inner')), may hold values from 0 to 15, all different within a row
- w_gate: bfloat16 [32, 4, 2048, 768], P(('group', 'inner')), may hold values from -0.125 to 0.125
- w_up: bfloat16 [32, 4, 2048, 768], P(('group', 'inner')), may hold values from -0.125 to 0.125
- w_down: bfloat16 [32, 4, 768, 2048], P(('group', 'inner')), may hold values from -0.21875 to 0.21875
Outputs:
- mixed: bfloat16 [1024, 2048], P(('group', 'inner'))
- grad_tokens: bfloat16 [1024, 2048], P(('group', 'inner'))
- grad_gate: bfloat16 [32, 4, 2048, 768], P(('group', 'inner'))
- grad_up: bfloat16 [32, 4, 2048, 768], P(('group', 'inner'))
- grad_down: bfloat16 [32, 4, 768, 2048], P(('group', 'inner'))
Inputs may be any that keep to these rules, and one draw needn't show every extreme that they name: `group_choice`: each token names 4 different routing groups. `pair_pick`: the picks of one token within one routing group differ.
All inputs are finite; a program needn't handle non-finite values.
Results may differ from a plain program's by a relative error of at most 0.015.
Values may be sent and summed in bfloat16 or wider, within the bound.
No kernel may reach another device: no remote copies, remote signals or barrier semaphores. Data moves between devices by JAX's collectives and lax.ppermute only.
A program may use at most 128 MiB of HBM per device.

v0:
```python
import jax
import jax.numpy as jnp
from jax import lax
from jax.sharding import PartitionSpec as P

EXPERTS = 128
TOPK = 8
RGROUPS = 8
CAP = 2


def expert_ids(group_choice, pair_pick):
    per_group = EXPERTS // RGROUPS
    joined = group_choice[:, :, None] * per_group + pair_pick
    return joined.reshape(joined.shape[0], TOPK)


def slot_table(ids, weights):
    flat = ids.reshape(-1)
    number = flat.shape[0]
    onehot = (flat[:, None] == jnp.arange(EXPERTS, dtype=jnp.int32)[None, :]).astype(jnp.int32)
    before = jnp.cumsum(onehot, axis=0) - onehot
    rank = jnp.sum(before * onehot, axis=1)
    target = jnp.where(rank < CAP, flat * CAP + rank, EXPERTS * CAP)
    owner = jnp.arange(number, dtype=jnp.int32) // TOPK
    empty = ids.shape[0]
    slot_token = jnp.full((EXPERTS * CAP + 1,), empty, jnp.int32).at[target].set(owner)[:-1]
    slot_weight = (
        jnp.zeros((EXPERTS * CAP + 1,), jnp.float32).at[target].set(weights.reshape(-1))[:-1]
    )
    return (slot_token, slot_weight)


def dispatch(rows, groups, inner, split, slots, width):
    local, owners, joined = rows.shape
    copies = jnp.broadcast_to(rows[:, :, None], (local, owners, split, joined))
    copies = copies.reshape(local, groups, inner, joined)
    received = lax.all_to_all(
        lax.all_to_all(copies, "group", split_axis=1, concat_axis=1, tiled=True),
        "inner",
        split_axis=2,
        concat_axis=2,
        tiled=True,
    )
    return received.reshape(local, groups * inner * slots, width)


def send_back(partial_value, groups, inner, split):
    local, total, width = partial_value.shape
    slots = total // (groups * inner)
    owners = groups * inner // split
    returned = lax.all_to_all(
        lax.all_to_all(
            partial_value.reshape(local, groups, inner, slots * width).astype(jnp.bfloat16),
            "group",
            split_axis=1,
            concat_axis=1,
            tiled=True,
        ),
        "inner",
        split_axis=2,
        concat_axis=2,
        tiled=True,
    ).astype(jnp.float32)
    returned = jnp.sum(returned.reshape(local, owners, split, slots * width), axis=2).astype(
        jnp.bfloat16
    )
    return returned.reshape(local * owners * slots, width)


def on_device(tokens, upstream, gate_weights, group_choice, pair_pick, w_gate, w_up, w_down):
    groups = lax.axis_size("group")
    inner = lax.axis_size("inner")
    devices = groups * inner
    local = w_gate.shape[1]
    split = devices * local // EXPERTS
    owners = devices // split
    count = tokens.shape[0]
    width = tokens.shape[1]
    ids = expert_ids(group_choice, pair_pick)
    slot_token, slot_weight = slot_table(ids, gate_weights)
    order_token = slot_token.reshape(owners, local, CAP).transpose(1, 0, 2).reshape(-1)
    order_weight = slot_weight.reshape(owners, local, CAP).transpose(1, 0, 2).reshape(-1)
    filler = jnp.zeros((1, width), tokens.dtype)
    x_pad = jnp.concatenate([tokens, filler], axis=0)
    dy_pad = jnp.concatenate([upstream, filler], axis=0)
    x_rows = x_pad[order_token].reshape(local, owners, CAP * width)
    x_recv = dispatch(x_rows, groups, inner, split, CAP, width)
    w_g = w_gate[0]
    w_u = w_up[0]
    w_d = w_down[0]
    gate = jnp.einsum("lrd,ldf->lrf", x_recv, w_g, preferred_element_type=jnp.float32)
    upv = jnp.einsum("lrd,ldf->lrf", x_recv, w_u, preferred_element_type=jnp.float32)
    sig = jax.nn.sigmoid(gate)
    act = gate * sig
    hidden = (act * upv).astype(jnp.bfloat16)
    out_partial = jnp.einsum("lrf,lfd->lrd", hidden, w_d, preferred_element_type=jnp.float32)
    out_values = send_back(out_partial, groups, inner, split)
    onehot = order_token[None, :] == jnp.arange(count, dtype=jnp.int32)[:, None]
    blend = jnp.where(onehot, order_weight[None, :], 0.0)
    mixed = jnp.dot(
        blend,
        out_values.astype(jnp.float32),
        precision=lax.Precision.HIGHEST,
        preferred_element_type=jnp.float32,
    ).astype(jnp.bfloat16)
    dout_rows = (order_weight[:, None] * dy_pad[order_token].astype(jnp.float32)).astype(
        jnp.bfloat16
    )
    dout = dispatch(dout_rows.reshape(local, owners, CAP * width), groups, inner, split, CAP, width)
    dh = jnp.einsum("lrd,lfd->lrf", dout, w_d, preferred_element_type=jnp.float32)
    dgate = (dh * upv * sig * (1.0 + gate * (1.0 - sig))).astype(jnp.bfloat16)
    dup = (dh * act).astype(jnp.bfloat16)
    dx_partial = jnp.einsum(
        "lrf,ldf->lrd", dgate, w_g, preferred_element_type=jnp.float32
    ) + jnp.einsum("lrf,ldf->lrd", dup, w_u, preferred_element_type=jnp.float32)
    grad_gate = jnp.einsum(
        "lrd,lrf->ldf", x_recv, dgate, preferred_element_type=jnp.float32
    ).astype(jnp.bfloat16)
    grad_up = jnp.einsum("lrd,lrf->ldf", x_recv, dup, preferred_element_type=jnp.float32).astype(
        jnp.bfloat16
    )
    grad_down = jnp.einsum("lrf,lrd->lfd", hidden, dout, preferred_element_type=jnp.float32).astype(
        jnp.bfloat16
    )
    dx_values = send_back(dx_partial, groups, inner, split)
    select = onehot.astype(jnp.bfloat16)
    grad_tokens = jnp.dot(select, dx_values, preferred_element_type=jnp.float32).astype(
        jnp.bfloat16
    )
    return (mixed, grad_tokens, grad_gate[None], grad_up[None], grad_down[None])


def solution(mesh):
    in_specs = (
        P(("group", "inner"), None),
        P(("group", "inner"), None),
        P(("group", "inner"), None),
        P(("group", "inner"), None),
        P(("group", "inner"), None, None),
        P(("group", "inner"), None, None, None),
        P(("group", "inner"), None, None, None),
        P(("group", "inner"), None, None, None),
    )
    out_specs = (
        P(("group", "inner"), None),
        P(("group", "inner"), None),
        P(("group", "inner"), None, None, None),
        P(("group", "inner"), None, None, None),
        P(("group", "inner"), None, None, None),
    )
    return jax.shard_map(
        on_device, mesh=mesh, in_specs=in_specs, out_specs=out_specs, check_vma=False
    )
```

profile of v0, /device:TPU:0, one launch (start us, length us, event | category | flops | bytes accessed | tf_op | source)
XLA Modules:
  0.0 251.0 jit_solution(15822448910543016260)
XLA Ops:
  0.7 0.7 broadcast_multiply_fusion.1
  1.4 0.7 broadcast_multiply_fusion
  2.2 0.1 eq.44
  2.4 0.1 eq.40
  2.6 0.2 mul.61
  2.9 0.2 fusion.23
  3.2 0.2 fusion.25
  3.4 1.4 scatter_custom_fusion
  4.8 0.2 reshape.135
  5.0 0.1 reshape.138
  5.1 0.9 concatenate.6
  6.1 1.4 gather_fusion
  7.4 0.4 reshape_broadcast_in_dim_reshape.4
  7.8 1.0 copy.54
  8.9 5.2 %all-to-all-start = ((bf16[4,4,8,4096]{3,2,0,1:T(8,128)(2,1)}), bf16[4,4,8,4096]{3,2,0,1:T(8,128)(2,1)}, u32[]{:S(2)}, u32[]{:S(2)}) async-start(bf16[4,4,8,4096]{3,2,0,1:T(8,128)(2,1)} %copy.54), calls=%async_computation | async-start | bytes 2097152 | tf_op jit(solution)/shard_map/all_to_all | solution.py:39
  14.2 1.4 scatter_custom_fusion.1
  15.6 0.2 reshape.137
  15.8 0.2 copy.61
  16.0 1.4 gather_fusion.1
  17.4 0.3 reshape.141
  17.7 0.2 mul.65
  17.9 1.3 fusion.21
  19.2 9.2 %all-to-all-done = bf16[4,4,8,4096]{3,2,0,1:T(8,128)(2,1)} async-done(((bf16[4,4,8,4096]{3,2,0,1:T(8,128)(2,1)}), bf16[4,4,8,4096]{3,2,0,1:T(8,128)(2,1)}, u32[]{:S(2)}, u32[]{:S(2)}) %all-to-all-start) | async-done | bytes 1048608 | tf_op jit(solution)/shard_map/all_to_all | solution.py:39
  28.3 3.5 %all-to-all-start.4 = ((bf16[4,4,8,4096]{3,2,0,1:T(8,128)(2,1)}), bf16[4,4,8,4096]{3,2,0,1:T(8,128)(2,1)S(1)}, u32[]{:S(2)}, u32[]{:S(2)}) async-start(bf16[4,4,8,4096]{3,2,0,1:T(8,128)(2,1)} %fusion.21), calls=%async_computation.4 | async-start | bytes 2097152 | tf_op jit(solution)/shard_map/all_to_all | solution.py:39
  31.8 3.0 %copy.55 = bf16[4,4,8,4096]{3,1,0,2:T(4,128)(2,1)} copy(bf16[4,4,8,4096]{3,2,0,1:T(8,128)(2,1)} %all-to-all-done) | data formatting | bytes 2097152 | tf_op jit(solution)/shard_map/all_to_all | solution.py:39
  34.9 10.3 %all-to-all-done.4 = bf16[4,4,8,4096]{3,2,0,1:T(8,128)(2,1)S(1)} async-done(((bf16[4,4,8,4096]{3,2,0,1:T(8,128)(2,1)}), bf16[4,4,8,4096]{3,2,0,1:T(8,128)(2,1)S(1)}, u32[]{:S(2)}, u32[]{:S(2)}) %all-to-all-start.4) | async-done | bytes 1048608 | tf_op jit(solution)/shard_map/all_to_all | solution.py:39
  45.2 4.9 %all-to-all-start.1 = ((bf16[4,4,8,4096]{3,1,0,2:T(4,128)(2,1)}), bf16[4,4,8,4096]{3,1,0,2:T(4,128)(2,1)S(1)}, u32[]{:S(2)}, u32[]{:S(2)}) async-start(bf16[4,4,8,4096]{3,1,0,2:T(4,128)(2,1)} %copy.55), calls=%async_computation.1 | async-start | bytes 2097152 | tf_op jit(solution)/shard_map/all_to_all | solution.py:38
  50.1 1.8 copy.63
  51.8 24.8 %all-to-all-done.1 = bf16[4,4,8,4096]{3,1,0,2:T(4,128)(2,1)S(1)} async-done(((bf16[4,4,8,4096]{3,1,0,2:T(4,128)(2,1)}), bf16[4,4,8,4096]{3,1,0,2:T(4,128)(2,1)S(1)}, u32[]{:S(2)}, u32[]{:S(2)}) %all-to-all-start.1) | async-done | bytes 1048608 | tf_op jit(solution)/shard_map/all_to_all | solution.py:38
  76.7 3.7 %all-to-all-start.5 = ((bf16[4,4,8,4096]{3,1,0,2:T(4,128)(2,1)}), bf16[4,4,8,4096]{3,1,0,2:T(4,128)(2,1)S(1)}, u32[]{:S(2)}, u32[]{:S(2)}) async-start(bf16[4,4,8,4096]{3,1,0,2:T(4,128)(2,1)} %copy.63), calls=%async_computation.5 | async-start | bytes 2097152 | tf_op jit(solution)/shard_map/all_to_all | solution.py:38
  80.4 1.6 copy.56
  82.0 1.4 reshape.139
  83.4 23.3 %all-to-all-done.5 = bf16[4,4,8,4096]{3,1,0,2:T(4,128)(2,1)S(1)} async-done(((bf16[4,4,8,4096]{3,1,0,2:T(4,128)(2,1)}), bf16[4,4,8,4096]{3,1,0,2:T(4,128)(2,1)S(1)}, u32[]{:S(2)}, u32[]{:S(2)}) %all-to-all-start.5) | async-done | bytes 1048608 | tf_op jit(solution)/shard_map/all_to_all | solution.py:38
  106.7 1.6 copy.64
  108.3 1.4 reshape.140
  109.7 6.6 %fusion.6 = f32[4,64,768]{2,1,0:T(8,128)S(1)} fusion(bf16[4,64,2048]{2,1,0:T(8,128)(2,1)S(1)} %reshape.139, bf16[1,4,2048,768]{3,2,1,0:T(8,128)(2,1)} %param.14), kind=kOutput, calls=%fused_computation.10 | convolution fusion | flops 805306368 | bytes 14417920 | tf_op jit(solution)/shard_map/lrd,ldf->lrf/dot_general | solution.py:93
  116.4 8.6 %fusion = f32[4,64,768]{2,1,0:T(8,128)S(1)} fusion(bf16[4,64,2048]{2,1,0:T(8,128)(2,1)S(1)} %reshape.140, bf16[1,4,768,2048]{3,2,1,0:T(8,128)(2,1)} %param.15), kind=kOutput, calls=%fused_computation.4 | convolution fusion | flops 805306368 | bytes 14417920 | tf_op jit(solution)/shard_map/lrd,lfd->lrf/dot_general | solution.py:111
  125.0 7.1 %multiply_convert_fusion.1 = (bf16[4,64,768]{2,1,0:T(8,128)(2,1)S(1)}, bf16[4,64,768]{2,1,0:T(8,128)(2,1)S(1)}, bf16[4,64,768]{2,1,0:T(8,128)(2,1)S(1)}) fusion(f32[4,64,768]{2,1,0:T(8,128)S(1)} %fusion, f32[4,64,768]{2,1,0:T(8,128)S(1)} %fusion.6, bf16[4,64,2048]{2,1,0:T(8,128)(2,1)S(1)} %reshape.139, bf16[1,4,2048,768]{3,2,1,0:T(8,128)(2,1)} %param.13), kind=kOutput, calls=%fused_computation.27 | convolution fusion | flops 808255488 | bytes 16384000 | tf_op jit(solution)/shard_map/lrd,ldf->lrf/dot_general | solution.py:92
  132.2 3.3 %fusion.18 = bf16[4,64,2048]{2,1,0:T(8,128)(2,1)} fusion(bf16[4,64,768]{2,1,0:T(8,128)(2,1)S(1)} %get-tuple-element.9, bf16[1,4,768,2048]{3,2,1,0:T(8,128)(2,1)S(1)} %bitcast.75), kind=kOutput, calls=%fused_computation.21 | convolution fusion | flops 805830656 | bytes 14024704 | tf_op jit(solution)/shard_map/lrf,lfd->lrd/dot_general | solution.py:97
  135.5 2.2 convert_element_type.72
  137.7 2.3 copy.57
  140.0 4.5 %all-to-all-start.2 = ((bf16[4,4,8,4096]{3,2,0,1:T(8,128)(2,1)}), bf16[4,4,8,4096]{3,2,0,1:T(8,128)(2,1)}, u32[]{:S(2)}, u32[]{:S(2)}) async-start(bf16[4,4,8,4096]{3,2,0,1:T(8,128)(2,1)} %copy.57), calls=%async_computation.2 | async-start | bytes 2097152 | tf_op jit(solution)/shard_map/all_to_all | solution.py:53
  144.5 8.4 %fusion.4 = f32[4,64,2048]{2,1,0:T(8,128)S(1)} fusion(bf16[4,64,768]{2,1,0:T(8,128)(2,1)S(1)} %get-tuple-element.8, bf16[1,4,2048,768]{3,2,1,0:T(8,128)(2,1)} %param.14), kind=kOutput, calls=%fused_computation.8 | convolution fusion | flops 805306368 | bytes 15073280 | tf_op jit(solution)/shard_map/lrf,ldf->lrd/dot_general | solution.py:116
  152.9 9.4 %fusion.15 = bf16[4,64,2048]{2,1,0:T(8,128)(2,1)} fusion(f32[4,64,2048]{2,1,0:T(8,128)S(1)} %fusion.4, bf16[4,64,768]{2,1,0:T(8,128)(2,1)S(1)} %get-tuple-element.7, bf16[1,4,2048,768]{3,2,1,0:T(8,128)(2,1)} %param.13), kind=kOutput, calls=%fused_computation.20 | convolution fusion | flops 806354944 | bytes 16121856 | tf_op jit(solution)/shard_map/lrf,ldf->lrd/dot_general | solution.py:114
  162.3 2.2 convert_element_type.81
  164.5 2.3 copy.65
  166.8 4.3 %all-to-all-start.6 = ((bf16[4,4,8,4096]{3,2,0,1:T(8,128)(2,1)}), bf16[4,4,8,4096]{3,2,0,1:T(8,128)(2,1)}, u32[]{:S(2)}, u32[]{:S(2)}) async-start(bf16[4,4,8,4096]{3,2,0,1:T(8,128)(2,1)} %copy.65), calls=%async_computation.6 | async-start | bytes 2097152 | tf_op jit(solution)/shard_map/all_to_all | solution.py:53
  171.1 3.0 %copy.58 = bf16[4,4,8,4096]{3,1,0,2:T(4,128)(2,1)} copy(bf16[4,4,8,4096]{3,2,0,1:T(8,128)(2,1)} %all-to-all-done.2) | data formatting | bytes 2097152 | tf_op jit(solution)/shard_map/all_to_all | solution.py:53
  174.1 10.8 %all-to-all-done.6 = bf16[4,4,8,4096]{3,2,0,1:T(8,128)(2,1)} async-done(((bf16[4,4,8,4096]{3,2,0,1:T(8,128)(2,1)}), bf16[4,4,8,4096]{3,2,0,1:T(8,128)(2,1)}, u32[]{:S(2)}, u32[]{:S(2)}) %all-to-all-start.6) | async-done | bytes 1048608 | tf_op jit(solution)/shard_map/all_to_all | solution.py:53
  184.9 4.2 %all-to-all-start.3 = ((bf16[4,4,8,4096]{3,1,0,2:T(4,128)(2,1)}), bf16[4,4,8,4096]{3,1,0,2:T(4,128)(2,1)}, u32[]{:S(2)}, u32[]{:S(2)}) async-start(bf16[4,4,8,4096]{3,1,0,2:T(4,128)(2,1)} %copy.58), calls=%async_computation.3 | async-start | bytes 2097152 | tf_op jit(solution)/shard_map/all_to_all | solution.py:52
  189.1 3.0 %copy.66 = bf16[4,4,8,4096]{3,1,0,2:T(4,128)(2,1)} copy(bf16[4,4,8,4096]{3,2,0,1:T(8,128)(2,1)} %all-to-all-done.6) | data formatting | bytes 2097152 | tf_op jit(solution)/shard_map/all_to_all | solution.py:53
  192.1 23.6 %all-to-all-done.3 = bf16[4,4,8,4096]{3,1,0,2:T(4,128)(2,1)} async-done(((bf16[4,4,8,4096]{3,1,0,2:T(4,128)(2,1)}), bf16[4,4,8,4096]{3,1,0,2:T(4,128)(2,1)}, u32[]{:S(2)}, u32[]{:S(2)}) %all-to-all-start.3) | async-done | bytes 1048608 | tf_op jit(solution)/shard_map/all_to_all | solution.py:52
  215.7 4.5 %all-to-all-start.7 = ((bf16[4,4,8,4096]{3,1,0,2:T(4,128)(2,1)}), bf16[4,4,8,4096]{3,1,0,2:T(4,128)(2,1)}, u32[]{:S(2)}, u32[]{:S(2)}) async-start(bf16[4,4,8,4096]{3,1,0,2:T(4,128)(2,1)} %copy.66), calls=%async_computation.7 | async-start | bytes 2097152 | tf_op jit(solution)/shard_map/all_to_all | solution.py:52
  220.2 0.1 eq.48
  220.5 6.6 %convert_bitcast_fusion = bf16[1,4,768,2048]{3,2,1,0:T(8,128)(2,1)} fusion(bf16[4,64,768]{2,1,0:T(8,128)(2,1)S(1)} %get-tuple-element.9, bf16[4,64,2048]{2,1,0:T(8,128)(2,1)S(1)} %reshape.140), kind=kOutput, calls=%fused_computation.16 | convolution fusion | flops 811597824 | bytes 14024704 | tf_op jit(solution)/shard_map/lrf,lrd->lfd/dot_general | solution.py:123
  227.2 6.6 %convert_bitcast_fusion.2 = bf16[1,4,2048,768]{3,2,1,0:T(8,128)(2,1)} fusion(bf16[4,64,2048]{2,1,0:T(8,128)(2,1)S(1)} %reshape.139, bf16[4,64,768]{2,1,0:T(8,128)(2,1)S(1)} %get-tuple-element.7), kind=kOutput, calls=%fused_computation.18 | convolution fusion | flops 811597824 | bytes 14024704 | tf_op jit(solution)/shard_map/lrd,lrf->ldf/dot_general | solution.py:117
  233.8 6.6 %convert_bitcast_fusion.1 = bf16[1,4,2048,768]{3,2,1,0:T(8,128)(2,1)} fusion(bf16[4,64,2048]{2,1,0:T(8,128)(2,1)S(1)} %reshape.139, bf16[4,64,768]{2,1,0:T(8,128)(2,1)S(1)} %get-tuple-element.8), kind=kOutput, calls=%fused_computation.17 | convolution fusion | flops 811597824 | bytes 14024704 | tf_op jit(solution)/shard_map/lrd,lrf->ldf/dot_general | solution.py:120
  240.4 1.8 copy.59
  242.2 0.4 convert_element_type.73
  242.6 4.0 %all-to-all-done.7 = bf16[4,4,8,4096]{3,1,0,2:T(4,128)(2,1)} async-done(((bf16[4,4,8,4096]{3,1,0,2:T(4,128)(2,1)}), bf16[4,4,8,4096]{3,1,0,2:T(4,128)(2,1)}, u32[]{:S(2)}, u32[]{:S(2)}) %all-to-all-start.7) | async-done | bytes 1048608 | tf_op jit(solution)/shard_map/all_to_all | solution.py:52
  246.6 1.8 copy.67
  248.4 0.4 convert_element_type.82
  248.8 0.9 convolution_convert_fusion
  249.7 1.3 convolution_convert_fusion.1
  (33 shorter events, 0.8 us)
Async XLA Ops:
  0.6 13.4 %copy-start.1 = (f32[32,8]{0,1:T(8,128)S(1)}, f32[32,8]{0,1:T(8,128)}, u32[]{:S(2)}) copy-start(f32[32,8]{0,1:T(8,128)} %param.10) | copy-start | bytes 3076
  0.6 15.3 %copy-start = (bf16[32,2048]{1,0:T(8,128)(2,1)S(1)}, bf16[32,2048]{1,0:T(8,128)(2,1)}, u32[]{:S(2)}) copy-start(bf16[32,2048]{1,0:T(8,128)(2,1)} %param.9) | copy-start | bytes 393220
  8.9 19.4 %all-to-all-start = ((bf16[4,4,8,4096]{3,2,0,1:T(8,128)(2,1)}), bf16[4,4,8,4096]{3,2,0,1:T(8,128)(2,1)}, u32[]{:S(2)}, u32[]{:S(2)}) async-start(bf16[4,4,8,4096]{3,2,0,1:T(8,128)(2,1)} %copy.54), calls=%async_computation | async-start | bytes 2097152 | tf_op jit(solution)/shard_map/all_to_all | solution.py:39
  28.3 16.9 %all-to-all-start.4 = ((bf16[4,4,8,4096]{3,2,0,1:T(8,128)(2,1)}), bf16[4,4,8,4096]{3,2,0,1:T(8,128)(2,1)S(1)}, u32[]{:S(2)}, u32[]{:S(2)}) async-start(bf16[4,4,8,4096]{3,2,0,1:T(8,128)(2,1)} %fusion.21), calls=%async_computation.4 | async-start | bytes 2097152 | tf_op jit(solution)/shard_map/all_to_all | solution.py:39
  45.2 31.5 %all-to-all-start.1 = ((bf16[4,4,8,4096]{3,1,0,2:T(4,128)(2,1)}), bf16[4,4,8,4096]{3,1,0,2:T(4,128)(2,1)S(1)}, u32[]{:S(2)}, u32[]{:S(2)}) async-start(bf16[4,4,8,4096]{3,1,0,2:T(4,128)(2,1)} %copy.55), calls=%async_computation.1 | async-start | bytes 2097152 | tf_op jit(solution)/shard_map/all_to_all | solution.py:38
  76.7 30.1 %all-to-all-start.5 = ((bf16[4,4,8,4096]{3,1,0,2:T(4,128)(2,1)}), bf16[4,4,8,4096]{3,1,0,2:T(4,128)(2,1)S(1)}, u32[]{:S(2)}, u32[]{:S(2)}) async-start(bf16[4,4,8,4096]{3,1,0,2:T(4,128)(2,1)} %copy.63), calls=%async_computation.5 | async-start | bytes 2097152 | tf_op jit(solution)/shard_map/all_to_all | solution.py:38
  116.4 15.8 %slice-start = ((s8[12582912]{0:T(1024)(128)(4,1)}), s8[4194304]{0:T(1024)(128)(4,1)S(1)}, s32[]{:S(2)}) async-start(s8[12582912]{0:T(1024)(128)(4,1)} %bitcast.74), calls=%async_computation.8 | async-start | bytes 8388608
  116.4 15.8 %slice-start.1 = ((s8[12582912]{0:T(1024)(128)(4,1)}), s8[4194304]{0:T(1024)(128)(4,1)S(1)}, s32[]{:S(2)}) async-start(s8[12582912]{0:T(1024)(128)(4,1)} %bitcast.74), calls=%async_computation.9 | async-start | bytes 8388608
  125.0 7.2 %slice-start.2 = ((s8[12582912]{0:T(1024)(128)(4,1)}), s8[4194304]{0:T(1024)(128)(4,1)S(1)}, s32[]{:S(2)}) async-start(s8[12582912]{0:T(1024)(128)(4,1)} %bitcast.74), calls=%async_computation.10 | async-start | bytes 8388608
  140.0 26.8 %all-to-all-start.2 = ((bf16[4,4,8,4096]{3,2,0,1:T(8,128)(2,1)}), bf16[4,4,8,4096]{3,2,0,1:T(8,128)(2,1)}, u32[]{:S(2)}, u32[]{:S(2)}) async-start(bf16[4,4,8,4096]{3,2,0,1:T(8,128)(2,1)} %copy.57), calls=%async_computation.2 | async-start | bytes 2097152 | tf_op jit(solution)/shard_map/all_to_all | solution.py:53
  166.8 18.1 %all-to-all-start.6 = ((bf16[4,4,8,4096]{3,2,0,1:T(8,128)(2,1)}), bf16[4,4,8,4096]{3,2,0,1:T(8,128)(2,1)}, u32[]{:S(2)}, u32[]{:S(2)}) async-start(bf16[4,4,8,4096]{3,2,0,1:T(8,128)(2,1)} %copy.65), calls=%async_computation.6 | async-start | bytes 2097152 | tf_op jit(solution)/shard_map/all_to_all | solution.py:53
  184.9 30.8 %all-to-all-start.3 = ((bf16[4,4,8,4096]{3,1,0,2:T(4,128)(2,1)}), bf16[4,4,8,4096]{3,1,0,2:T(4,128)(2,1)}, u32[]{:S(2)}, u32[]{:S(2)}) async-start(bf16[4,4,8,4096]{3,1,0,2:T(4,128)(2,1)} %copy.58), calls=%async_computation.3 | async-start | bytes 2097152 | tf_op jit(solution)/shard_map/all_to_all | solution.py:52
  215.7 30.8 %all-to-all-start.7 = ((bf16[4,4,8,4096]{3,1,0,2:T(4,128)(2,1)}), bf16[4,4,8,4096]{3,1,0,2:T(4,128)(2,1)}, u32[]{:S(2)}, u32[]{:S(2)}) async-start(bf16[4,4,8,4096]{3,1,0,2:T(4,128)(2,1)} %copy.66), calls=%async_computation.7 | async-start | bytes 2097152 | tf_op jit(solution)/shard_map/all_to_all | solution.py:52
where the time goes:
time: 252 us; the launch traced here: 251 us
  waiting for transfers between devices  106 us (42%)
  matrix products  65.6 us (26%)
  local copies, waits for them, and re-layouts  40.5 us (16%)
  starting transfers between devices  34.8 us (14%)
  other arithmetic  3.13 us (1%)
    all_to_all x2, waiting for transfers between devices, dispatch(): lax.all_to_all(lax.all_to_all(copies, 'group', split_axis=1, concat_axis=...  48.2 us
    all_to_all x2, waiting for transfers between devices, send_back(): lax.all_to_all(lax.all_to_all(partial_value.reshape(local, groups, inner,...  27.6 us
    all_to_all x2, waiting for transfers between devices, dispatch(): lax.all_to_all(copies, 'group', split_axis=1, concat_axis=1, tiled=True)  19.5 us
    all_to_all x2, waiting for transfers between devices, send_back(): lax.all_to_all(partial_value.reshape(local, groups, inner, slots * width)...  10.8 us
    dot_general x1, matrix products, on_device(): jnp.einsum('lrf,ldf->lrd', dgate, w_g, preferred_element_type=jnp.float32)  9.44 us
    convert_element_type x4, local copies, waits for them, and re-layouts, send_back(): partial_value.reshape(local, groups, inner, slots * width)  8.96 us
    all_to_all x2, starting transfers between devices, send_back(): lax.all_to_all(lax.all_to_all(partial_value.reshape(local, groups, inner,...  8.74 us
    all_to_all x2, starting transfers between devices, send_back(): lax.all_to_all(partial_value.reshape(local, groups, inner, slots * width)...  8.72 us
  transfers between devices with their start and end apart: 8, of which 7 were waited for; matrix products, arithmetic and copies ran while one was open for 25% of the time, Pallas kernels for 0%

commit v1 on v0

--- a/solution.py
+++ b/solution.py
@@ -1,7 +1,12 @@
+import functools
+
 import jax
 import jax.numpy as jnp
 from jax import lax
+from jax.experimental import pallas as pl
+from jax.experimental.pallas import tpu as pltpu
 from jax.sharding import PartitionSpec as P
+
 
 EXPERTS = 128
 TOPK = 8
@@ -68,7 +73,7 @@
     return returned.reshape(local * owners * slots, width)
 
 
-def on_device(tokens, upstream, gate_weights, group_choice, pair_pick, w_gate, w_up, w_down):
+def on_device_general(tokens, upstream, gate_weights, group_choice, pair_pick, w_gate, w_up, w_down):
     groups = lax.axis_size("group")
     inner = lax.axis_size("inner")
     devices = groups * inner
@@ -131,7 +136,307 @@
     return (mixed, grad_tokens, grad_gate[None], grad_up[None], grad_down[None])
 
 
+COLUMNS = 4
+PLACES = 8
+TABLE = 128
+MIB = 1024 * 1024
+
+
+def params(mib, rank=0):
+    return pltpu.CompilerParams(
+        vmem_limit_bytes=mib * MIB,
+        dimension_semantics=("arbitrary",) * rank if rank else None,
+    )
+
+
+def cost(flops, moved):
+    return pl.CostEstimate(flops=int(flops), bytes_accessed=int(moved), transcendentals=0)
+
+
+def swap(value, axis, size, mask):
+    return lax.ppermute(value, axis, [(k, k ^ mask) for k in range(size)])
+
+
+def whole():
+    return pl.BlockSpec(memory_space=pltpu.VMEM)
+
+
+def select_tokens_kernel(local, count, width, place_ref, *refs):
+    pieces, rest = refs[:PLACES], refs[PLACES:]
+    near, rest = rest[: PLACES // 2], rest[PLACES // 2 :]
+    far, rest = rest[0], rest[1:]
+    outs, (pick_ref, pick_t_ref, high_ref, low_ref, scale_ref), full = rest[:COLUMNS], rest[COLUMNS:-1], rest[-1]
+    total = PLACES * count
+    rows = COLUMNS * local * PLACES * CAP
+    tables = []
+    for j in range(PLACES):
+        full[j * count : (j + 1) * count, :] = pieces[j][...]
+        tables.append(far[j // 2] if j % 2 else near[j // 2][...])
+    table = jnp.concatenate(tables, axis=0)
+    row = lax.broadcasted_iota(jnp.int32, (1, rows), 1)
+    slot = row % CAP
+    piece = row // CAP % PLACES
+    column = place_ref[0] ^ (row // (CAP * PLACES * local))
+    expert = (column * PLACES + place_ref[1]) * local + row // (CAP * PLACES) % local
+    expert = expert.astype(jnp.float32)
+    member = jnp.zeros((total, rows), jnp.float32)
+    weight = jnp.zeros((total, rows), jnp.float32)
+    for k in range(TOPK):
+        same = table[:, k : k + 1] == expert
+        value = table[:, TOPK + k : TOPK + k + 1]
+        member = jnp.where(same, 1.0, member)
+        weight = jnp.where(same, value, weight)
+    token = lax.broadcasted_iota(jnp.int32, (total, 1), 0)
+    other = lax.broadcasted_iota(jnp.int32, (1, total), 1)
+    earlier = ((other < token) & (other // count == token // count)).astype(jnp.float32)
+    rank = jnp.dot(
+        earlier.astype(jnp.bfloat16), member.astype(jnp.bfloat16), preferred_element_type=jnp.float32
+    )
+    kept = (member > 0.5) & (rank == slot.astype(jnp.float32)) & (token // count == piece)
+    pick_t = jnp.where(kept, 1.0, 0.0)
+    weight = jnp.where(kept, weight, 0.0)
+    high = weight.astype(jnp.bfloat16)
+    pick = pick_t.T.astype(jnp.bfloat16)
+    pick_ref[...] = pick
+    pick_t_ref[...] = pick_t.astype(jnp.bfloat16)
+    high_ref[...] = high
+    low_ref[...] = (weight - high.astype(jnp.float32)).astype(jnp.bfloat16)
+    scale_ref[...] = jnp.sum(weight.T, axis=1, keepdims=True)
+    chosen = jnp.dot(pick, full[...], preferred_element_type=jnp.float32).astype(jnp.bfloat16)
+    part = rows // COLUMNS
+    for m in range(COLUMNS):
+        outs[m][...] = chosen[m * part : (m + 1) * part].reshape(outs[m].shape)
+
+
+def select_upstream_kernel(count, pick_ref, scale_ref, *refs):
+    pieces, outs, full = refs[:PLACES], refs[PLACES:-1], refs[-1]
+    for j in range(PLACES):
+        full[j * count : (j + 1) * count, :] = pieces[j][...]
+    chosen = jnp.dot(pick_ref[...], full[...], preferred_element_type=jnp.float32)
+    chosen = (chosen * scale_ref[...]).astype(jnp.bfloat16)
+    part = chosen.shape[0] // COLUMNS
+    for m in range(COLUMNS):
+        outs[m][...] = chosen[m * part : (m + 1) * part].reshape(outs[m].shape)
+
+
+def combine_kernel(count, terms, *refs):
+    blends, pieces, (even_ref, odd_ref, full) = refs[:terms], refs[terms : terms + COLUMNS], refs[terms + COLUMNS :]
+    width = full.shape[1]
+    part = full.shape[0] // COLUMNS
+    for m in range(COLUMNS):
+        full[m * part : (m + 1) * part, :] = pieces[m][...].reshape(part, width)
+    value = jnp.dot(blends[0][...], full[...], preferred_element_type=jnp.float32)
+    for blend in blends[1:]:
+        value = value + jnp.dot(blend[...], full[...], preferred_element_type=jnp.float32)
+    value = value.astype(jnp.bfloat16)
+    for j in range(PLACES):
+        target = odd_ref if j % 2 else even_ref
+        target[j // 2] = value[j * count : (j + 1) * count]
+
+
+def across(a, b):
+    return lax.dot_general(a, b, (((1,), (1,)), ((), ())), preferred_element_type=jnp.float32)
+
+
+def down(a, b):
+    return lax.dot_general(a, b, (((0,), (0,)), ((), ())), preferred_element_type=jnp.float32)
+
+
+def joined(pieces, e):
+    return jnp.concatenate([piece[e] for piece in pieces], axis=0)
+
+
+def forward_kernel(*refs):
+    pieces = refs[:COLUMNS]
+    wg_ref, wu_ref, wd_ref, g_ref, u_ref, h_ref = refs[COLUMNS : COLUMNS + 6]
+    outs = refs[COLUMNS + 6 :]
+    part = outs[0].shape[1]
+
+    @pl.loop(0, wg_ref.shape[1])
+    def _(e):
+        rows = joined(pieces, e)
+        g = jnp.dot(rows, wg_ref[0, e], preferred_element_type=jnp.float32)
+        u = jnp.dot(rows, wu_ref[0, e], preferred_element_type=jnp.float32)
+        h = (g * jax.nn.sigmoid(g) * u).astype(jnp.bfloat16)
+        g_ref[e] = g
+        u_ref[e] = u
+        h_ref[e] = h
+        value = jnp.dot(h, wd_ref[0, e], preferred_element_type=jnp.float32).astype(jnp.bfloat16)
+        for m in range(COLUMNS):
+            outs[m][e] = value[m * part : (m + 1) * part]
+
+
+def backward_kernel(*refs):
+    pieces = refs[:COLUMNS]
+    g_ref, u_ref, wg_ref, wu_ref, wd_ref, dg_ref, du_ref = refs[COLUMNS : COLUMNS + 7]
+    outs = refs[COLUMNS + 7 :]
+    part = outs[0].shape[1]
+
+    @pl.loop(0, wg_ref.shape[1])
+    def _(e):
+        dh = across(joined(pieces, e), wd_ref[0, e])
+        g = g_ref[e]
+        sig = jax.nn.sigmoid(g)
+        dg = (dh * u_ref[e] * sig * (1.0 + g * (1.0 - sig))).astype(jnp.bfloat16)
+        du = (dh * (g * sig)).astype(jnp.bfloat16)
+        dg_ref[e] = dg
+        du_ref[e] = du
+        value = (across(dg, wg_ref[0, e]) + across(du, wu_ref[0, e])).astype(jnp.bfloat16)
+        for m in range(COLUMNS):
+            outs[m][e] = value[m * part : (m + 1) * part]
+
+
+def up_grads_kernel(*refs):
+    pieces = refs[:COLUMNS]
+    dg_ref, du_ref, gg_ref, gu_ref = refs[COLUMNS:]
+    rows = joined(pieces, 0)
+    gg_ref[0, 0] = down(rows, dg_ref[0]).astype(jnp.bfloat16)
+    gu_ref[0, 0] = down(rows, du_ref[0]).astype(jnp.bfloat16)
+
+
+def down_grads_kernel(*refs):
+    pieces = refs[:COLUMNS]
+    h_ref, gd_ref = refs[COLUMNS:]
+    gd_ref[0, 0] = down(h_ref[0], joined(pieces, 0)).astype(jnp.bfloat16)
+
+
+def after(value, *others):
+    return lax.optimization_barrier((value, *others))[0]
+
+
+def on_device(tokens, upstream, gate_weights, group_choice, pair_pick, w_gate, w_up, w_down):
+    count, width = tokens.shape
+    local, hidden = w_gate.shape[1], w_gate.shape[3]
+    rows = COLUMNS * local * PLACES * CAP
+    part = PLACES * CAP
+    bf16, f32 = jnp.bfloat16, jnp.float32
+
+    def along(value):
+        return [value] + [swap(value, "inner", PLACES, 2 * z) for z in (1, 2, 3)]
+
+    def both(near):
+        return [one for z in near for one in (z, swap(z, "inner", PLACES, 1))]
+
+    def exchange(pieces):
+        return [pieces[0]] + [swap(pieces[m], "group", COLUMNS, m) for m in (1, 2, 3)]
+
+    ids = expert_ids(group_choice, pair_pick)
+    blank = jnp.zeros((count, TABLE - 2 * TOPK), f32)
+    table = jnp.concatenate([ids.astype(f32), gate_weights, blank], axis=1)
+    x_near = along(tokens)
+    table_near = along(table)
+    table_far = swap(jnp.stack(table_near), "inner", PLACES, 1)
+
+    sent = [jax.ShapeDtypeStruct((local, part, width), bf16)] * COLUMNS
+    square = jax.ShapeDtypeStruct((rows, rows), bf16)
+    place = jnp.stack([lax.axis_index("group"), lax.axis_index("inner")]).astype(jnp.int32)
+    *x_send, pick, pick_t, high, low, scale = pl.pallas_call(
+        functools.partial(select_tokens_kernel, local, count, width),
+        name="select_tokens",
+        out_shape=sent + [square] * 4 + [jax.ShapeDtypeStruct((rows, 1), f32)],
+        in_specs=[pl.BlockSpec(memory_space=pltpu.SMEM)] + [whole()] * (PLACES + PLACES // 2 + 1),
+        out_specs=[whole()] * (COLUMNS + 5),
+        scratch_shapes=[pltpu.VMEM((PLACES * count, width), bf16)],
+        compiler_params=params(8),
+        cost_estimate=cost(2 * rows * rows * width, 4 * rows * width),
+    )(place, *both(x_near), *table_near, table_far)
+    x_recv = exchange(x_send)
+
+    dy_near = along(after(upstream, *x_near[1:]))
+    dy_send = pl.pallas_call(
+        functools.partial(select_upstream_kernel, count),
+        name="select_upstream",
+        out_shape=sent,
+        in_specs=[whole()] * (PLACES + 2),
+        out_specs=[whole()] * COLUMNS,
+        scratch_shapes=[pltpu.VMEM((PLACES * count, width), bf16)],
+        compiler_params=params(8),
+        cost_estimate=cost(2 * rows * rows * width, 4 * rows * width),
+    )(pick, scale, *both(dy_near))
+    dy_recv = exchange(dy_send)
+
+    hid = lambda t: jax.ShapeDtypeStruct((local, rows // local, hidden), t)
+    weight_bytes = 2 * local * width * hidden
+    flops = 2 * rows * width * hidden
+
+    g, u, h, *out_send = pl.pallas_call(
+        forward_kernel,
+        name="forward",
+        out_shape=[hid(f32), hid(f32), hid(bf16)] + sent,
+        in_specs=[whole()] * (COLUMNS + 3),
+        out_specs=[whole()] * (COLUMNS + 3),
+        compiler_params=params(8),
+        cost_estimate=cost(12 * flops, 3 * weight_bytes),
+    )(after(x_recv[0], *dy_send), *x_recv[1:], w_gate, w_up, w_down)
+    out_back = exchange(out_send)
+
+    dg, du, *dx_send = pl.pallas_call(
+        backward_kernel,
+        name="backward",
+        out_shape=[hid(bf16), hid(bf16)] + sent,
+        in_specs=[whole()] * (COLUMNS + 5),
+        out_specs=[whole()] * (COLUMNS + 2),
+        compiler_params=params(8),
+        cost_estimate=cost(12 * flops, 3 * weight_bytes),
+    )(*dy_recv, g, u, w_gate, w_up, w_down)
+    dx_back = exchange(dx_send)
+
+    def combine(blends, pieces, name):
+        half = jax.ShapeDtypeStruct((PLACES // 2, count, width), bf16)
+        even, odd = pl.pallas_call(
+            functools.partial(combine_kernel, count, len(blends)),
+            name=name,
+            out_shape=[half, half],
+            in_specs=[whole()] * (len(blends) + COLUMNS),
+            out_specs=[whole()] * 2,
+            scratch_shapes=[pltpu.VMEM((rows, width), bf16)],
+            compiler_params=params(8),
+            cost_estimate=cost(2 * rows * rows * width, 4 * rows * width),
+        )(*blends, *pieces)
+        other = swap(odd, "inner", PLACES, 1)
+        sums = [even[z].astype(f32) + other[z].astype(f32) for z in range(PLACES // 2)]
+        return sums[0], [sums[z].astype(bf16) for z in (1, 2, 3)]
+
+    def finish(total, parts):
+        for z in (1, 2, 3):
+            total = total + swap(parts[z - 1], "inner", PLACES, 2 * z).astype(f32)
+        return total.astype(bf16)
+
+    slot_spec = pl.BlockSpec((1, part, width), lambda e: (e, 0, 0))
+    hid_spec = pl.BlockSpec((1, rows // local, hidden), lambda e: (e, 0, 0))
+    up_spec = pl.BlockSpec((1, 1, width, hidden), lambda e: (0, e, 0, 0))
+    down_spec = pl.BlockSpec((1, 1, hidden, width), lambda e: (0, e, 0, 0))
+
+    out_own, out_parts = combine([high, low], [after(out_back[0], *dx_send)] + out_back[1:], "combine_out")
+    mixed = finish(out_own, out_parts)
+    grad_down = pl.pallas_call(
+        down_grads_kernel,
+        name="down_grads",
+        grid=(local,),
+        out_shape=jax.ShapeDtypeStruct(w_down.shape, bf16),
+        in_specs=[slot_spec] * COLUMNS + [hid_spec],
+        out_specs=down_spec,
+        compiler_params=params(32, 1),
+        cost_estimate=cost(4 * flops, weight_bytes),
+    )(*dy_recv, after(h, *out_parts))
+
+    dx_own, dx_parts = combine([pick_t], [after(dx_back[0], grad_down)] + dx_back[1:], "combine_dx")
+    grad_tokens = finish(dx_own, dx_parts)
+    grad_gate, grad_up = pl.pallas_call(
+        up_grads_kernel,
+        name="up_grads",
+        grid=(local,),
+        out_shape=[jax.ShapeDtypeStruct(w.shape, bf16) for w in (w_gate, w_up)],
+        in_specs=[slot_spec] * COLUMNS + [hid_spec] * 2,
+        out_specs=[up_spec, up_spec],
+        compiler_params=params(32, 1),
+        cost_estimate=cost(8 * flops, 2 * weight_bytes),
+    )(*x_recv, after(dg, *dx_parts), du)
+    return (mixed, grad_tokens, grad_gate, grad_up, grad_down)
+
+
 def solution(mesh):
+    ours = mesh.shape["group"] == COLUMNS and mesh.shape["inner"] == PLACES
     in_specs = (
         P(("group", "inner"), None),
         P(("group", "inner"), None),
@@ -150,5 +455,5 @@
         P(("group", "inner"), None, None, None),
     )
     return jax.shard_map(
-        on_device, mesh=mesh, in_specs=in_specs, out_specs=out_specs, check_vma=False
-    )
+        on_device if ours else on_device_general, mesh=mesh, in_specs=in_specs, out_specs=out_specs, check_vma=False
+    )

time: 252 us -> 134 us (0.53)
  waiting for transfers between devices: 106 us -> 19.5 us
  matrix products: 65.6 us -> 0 us
  Pallas kernels: 0 us -> 40.2 us
  local copies, waits for them, and re-layouts: 40.5 us -> 25.6 us
  starting transfers between devices: 34.8 us -> 44.3 us
    all_to_all x8 -> x0, waiting for transfers between devices: 106 us -> none  [the longest x2 48.2 us: dispatch(): lax.all_to_all(lax.all_to_all(copies, 'group', split_axis=1, concat_axis=...]
    dot_general x11 -> x0, matrix products: 65.6 us -> none  [the longest x1 9.44 us: on_device(): jnp.einsum('lrf,ldf->lrd', dgate, w_g, preferred_element_type=jnp.float32)]
    ppermute x0 -> x38, starting transfers between devices: none -> 44.3 us  [swap(): return lax.ppermute(value, axis, [(k, k ^ mask) for k in range(size)])]
    pallas_call x0 -> x8, Pallas kernels: none -> 40.2 us  [the longest x1 13.5 us: on_device(): pl.pallas_call(backward_kernel, name='backward', out_shape=[hid(bf16), hi...]
    all_to_all x8 -> x0, starting transfers between devices: 34.8 us -> none  [the longest x2 8.74 us: send_back(): lax.all_to_all(lax.all_to_all(partial_value.reshape(local, groups, inner,...]
    unnamed x12 -> x17, local copies, waits for them, and re-layouts: 0.11 us -> 25.4 us
    ppermute x0 -> x38, waiting for transfers between devices: none -> 19.5 us  [swap(): return lax.ppermute(value, axis, [(k, k ^ mask) for k in range(size)])]
    all_to_all x8 -> x0, local copies, waits for them, and re-layouts: 17.5 us -> none  [the longest x2 6.01 us: send_back(): lax.all_to_all(partial_value.reshape(local, groups, inner, slots * width)...]
  transfers between devices with their start and end apart: 8 -> 38, of which waited for: 7 -> 10; matrix products, arithmetic and copies ran while one was open for 25% -> 3% of each run, Pallas kernels for 0% -> 30%
where the time goes in v1:
time: 134 us
  starting transfers between devices  44.3 us (33%)
  Pallas kernels  40.2 us (30%)
  local copies, waits for them, and re-layouts  25.6 us (19%)
  waiting for transfers between devices  19.5 us (15%)
  other arithmetic  3.28 us (2%)
    ppermute x38, starting transfers between devices, swap(): return lax.ppermute(value, axis, [(k, k ^ mask) for k in range(size)])  44.3 us
    unnamed x17, local copies, waits for them, and re-layouts  25.4 us
    ppermute x38, waiting for transfers between devices, swap(): return lax.ppermute(value, axis, [(k, k ^ mask) for k in range(size)])  19.5 us
    pallas_call x1, Pallas kernels, on_device(): pl.pallas_call(backward_kernel, name='backward', out_shape=[hid(bf16), hi...  13.5 us
    pallas_call x1, Pallas kernels, on_device(): pl.pallas_call(up_grads_kernel, name='up_grads', grid=(local,), out_shape...  9.86 us
    pallas_call x1, Pallas kernels, on_device(): pl.pallas_call(forward_kernel, name='forward', out_shape=[hid(f32), hid(f...  7.14 us
    pallas_call x1, Pallas kernels, on_device(): pl.pallas_call(down_grads_kernel, name='down_grads', grid=(local,), out_s...  6.36 us
  transfers between devices with their start and end apart: 38, of which 10 were waited for; matrix products, arithmetic and copies ran while one was open for 3% of the time, Pallas kernels for 30%

profile of v1, /device:TPU:0, one launch (start us, length us, event | category | flops | bytes accessed | tf_op | source)
XLA Modules:
  0.0 133.7 jit_solution(10715533540553155888)
XLA Ops:
  0.6 4.1 %collective-permute-start.3 = (bf16[32,2048]{1,0:T(8,128)(2,1)}, bf16[32,2048]{1,0:T(8,128)(2,1)S(1)}, u32[]{:S(2)}, u32[]{:S(2)}) collective-permute-start(bf16[32,2048]{1,0:T(8,128)(2,1)} %refs_0_.1), channel_id=1, source_target_pairs={{0,4},{1,5},{2,6},{3,7},{4,0},{5,1},{6,2},{7,3},{8,12},{9,13},{10,... | collective-permute-start | bytes 393224 | tf_op jit(solution)/shard_map/ppermute | solution.py:157
  4.7 0.7 broadcast_multiply_fusion
  5.4 0.7 add_convert_fusion.6
  6.1 0.1 copy.15
  6.2 0.8 copy.16
  7.0 0.1 pad.6.clone
  7.0 0.1 maximum_maximum_fusion.refs_8_
  7.1 1.3 %collective-permute-start.9 = (f32[32,128]{1,0:T(8,128)S(1)}, f32[32,128]{1,0:T(8,128)S(1)}, u32[]{:S(2)}, u32[]{:S(2)}) collective-permute-start(f32[32,128]{1,0:T(8,128)S(1)} %maximum_maximum_fusion.refs_8_), channel_id=1, source_target_pairs={{0,6},{1,7},{2,4},{3,5},{4,2},{5,3},{6,0},{7,1},{8,14},{9,15},{10,... | collective-permute-start | bytes 49160 | tf_op jit(solution)/shard_map/ppermute | solution.py:157
  8.5 1.7 %collective-permute-start.8 = (f32[32,128]{1,0:T(8,128)S(1)}, f32[32,128]{1,0:T(8,128)S(1)}, u32[]{:S(2)}, u32[]{:S(2)}) collective-permute-start(f32[32,128]{1,0:T(8,128)S(1)} %maximum_maximum_fusion.refs_8_), channel_id=1, source_target_pairs={{0,4},{1,5},{2,6},{3,7},{4,0},{5,1},{6,2},{7,3},{8,12},{9,13},{10,... | collective-permute-start | bytes 49160 | tf_op jit(solution)/shard_map/ppermute | solution.py:157
  10.1 1.3 %collective-permute-start.7 = (f32[32,128]{1,0:T(8,128)S(1)}, f32[32,128]{1,0:T(8,128)S(1)}, u32[]{:S(2)}, u32[]{:S(2)}) collective-permute-start(f32[32,128]{1,0:T(8,128)S(1)} %maximum_maximum_fusion.refs_8_), channel_id=1, source_target_pairs={{0,2},{1,3},{2,0},{3,1},{4,6},{5,7},{6,4},{7,5},{8,10},{9,11},{10,... | collective-permute-start | bytes 49160 | tf_op jit(solution)/shard_map/ppermute | solution.py:157
  11.5 0.7 collective-permute-start.1
  12.2 3.2 %collective-permute-start.5 = (bf16[32,2048]{1,0:T(8,128)(2,1)}, bf16[32,2048]{1,0:T(8,128)(2,1)S(1)}, u32[]{:S(2)}, u32[]{:S(2)}) collective-permute-start(bf16[32,2048]{1,0:T(8,128)(2,1)} %refs_0_.1), channel_id=1, source_target_pairs={{0,6},{1,7},{2,4},{3,5},{4,2},{5,3},{6,0},{7,1},{8,14},{9,15},{10,... | collective-permute-start | bytes 393224 | tf_op jit(solution)/shard_map/ppermute | solution.py:157
  15.5 4.0 %collective-permute-done.1.refs_2_ = bf16[32,2048]{1,0:T(8,128)(2,1)S(1)} collective-permute-done((bf16[32,2048]{1,0:T(8,128)(2,1)}, bf16[32,2048]{1,0:T(8,128)(2,1)S(1)}, u32[]{:S(2)}, u32[]{:S(2)}) %collective-permute-start.1) | collective-permute-done | bytes 131104 | tf_op jit(solution)/shard_map/ppermute | solution.py:157
  19.5 3.4 %collective-permute-start.16 = (bf16[32,2048]{1,0:T(8,128)(2,1)}, bf16[32,2048]{1,0:T(8,128)(2,1)S(1)}, u32[]{:S(2)}, u32[]{:S(2)}) collective-permute-start(bf16[32,2048]{1,0:T(8,128)(2,1)} %refs_0_.2), channel_id=1, source_target_pairs={{0,6},{1,7},{2,4},{3,5},{4,2},{5,3},{6,0},{7,1},{8,14},{9,15},{10,... | collective-permute-start | bytes 393224 | tf_op jit(solution)/shard_map/ppermute | solution.py:157
  22.9 0.5 collective-permute-start.2
  23.4 0.1 collective-permute-start.10
  23.5 1.2 collective-permute-done.10.refs_12_
  24.7 0.2 collective-permute-start.6
  24.9 0.2 collective-permute-start.14
  25.1 0.9 collective-permute-start.12
  26.0 1.8 %collective-permute-done.16.refs_6_ = bf16[32,2048]{1,0:T(8,128)(2,1)S(1)} collective-permute-done((bf16[32,2048]{1,0:T(8,128)(2,1)}, bf16[32,2048]{1,0:T(8,128)(2,1)S(1)}, u32[]{:S(2)}, u32[]{:S(2)}) %collective-permute-start.16) | collective-permute-done | bytes 131104 | tf_op jit(solution)/shard_map/ppermute | solution.py:157
  27.9 0.9 copy-done.6
  28.8 1.8 %select_tokens.1 = (bf16[4,16,2048]{2,1,0:T(8,128)(2,1)S(1)}, bf16[4,16,2048]{2,1,0:T(8,128)(2,1)S(1)}, bf16[4,16,2048]{2,1,0:T(8,128)(2,1)S(1)}, bf16[4,16,2048...) custom-call(s32[2]{0:T(128)S(1)} %pad_add_fusion.place_ref, ...), custom_call_target="tpu_custom_call" | custom-call | flops 268435456 | bytes 2097152 | tf_op jit(solution)/shard_map/select_tokens/pallas_call | solution.py:333
  30.6 1.6 %collective-permute-start.18 = (bf16[4,16,2048]{2,1,0:T(8,128)(2,1)S(1)}, bf16[4,16,2048]{2,1,0:T(8,128)(2,1)S(1)}, u32[]{:S(2)}, u32[]{:S(2)}) collective-permute-start(bf16[4,16,2048]{2,1,0:T(8,128)(2,1)S(1)} %get-tuple-element.54), channel_id=1, source_target_pairs={{0,8},{8,0},{16,24},{24,16},{1,9},{9,1},{17,25},{25,17},{2,10},{10... | collective-permute-start | bytes 786440 | tf_op jit(solution)/shard_map/ppermute | solution.py:157
  32.2 2.3 %collective-permute-done.14.refs_4_ = bf16[32,2048]{1,0:T(8,128)(2,1)S(1)} collective-permute-done((bf16[32,2048]{1,0:T(8,128)(2,1)}, bf16[32,2048]{1,0:T(8,128)(2,1)S(1)}, u32[]{:S(2)}, u32[]{:S(2)}) %collective-permute-start.14) | collective-permute-done | bytes 131104 | tf_op jit(solution)/shard_map/ppermute | solution.py:157
  34.4 1.5 %collective-permute-start.19 = (bf16[4,16,2048]{2,1,0:T(8,128)(2,1)S(1)}, bf16[4,16,2048]{2,1,0:T(8,128)(2,1)S(1)}, u32[]{:S(2)}, u32[]{:S(2)}) collective-permute-start(bf16[4,16,2048]{2,1,0:T(8,128)(2,1)S(1)} %get-tuple-element.55), channel_id=1, source_target_pairs={{0,16},{8,24},{16,0},{24,8},{1,17},{9,25},{17,1},{25,9},{2,18},{10... | collective-permute-start | bytes 786440 | tf_op jit(solution)/shard_map/ppermute | solution.py:157
  36.0 1.4 %collective-permute-start.20 = (bf16[4,16,2048]{2,1,0:T(8,128)(2,1)S(1)}, bf16[4,16,2048]{2,1,0:T(8,128)(2,1)S(1)}, u32[]{:S(2)}, u32[]{:S(2)}) collective-permute-start(bf16[4,16,2048]{2,1,0:T(8,128)(2,1)S(1)} %get-tuple-element.56), channel_id=1, source_target_pairs={{0,24},{8,16},{16,8},{24,0},{1,25},{9,17},{17,9},{25,1},{2,26},{10... | collective-permute-start | bytes 786440 | tf_op jit(solution)/shard_map/ppermute | solution.py:157
  37.4 0.5 collective-permute-start.13
  37.9 0.8 collective-permute-done.15.refs_5_
  38.7 0.2 collective-permute-done.13.refs_3_
  38.9 0.9 copy-done.7
  39.8 0.4 select_upstream.1
  40.3 0.6 collective-permute-start.21
  40.9 1.5 %collective-permute-start.22 = (bf16[4,16,2048]{2,1,0:T(8,128)(2,1)S(1)}, bf16[4,16,2048]{2,1,0:T(8,128)(2,1)S(1)}, u32[]{:S(2)}, u32[]{:S(2)}) collective-permute-start(bf16[4,16,2048]{2,1,0:T(8,128)(2,1)S(1)} %get-tuple-element.51), channel_id=1, source_target_pairs={{0,16},{8,24},{16,0},{24,8},{1,17},{9,25},{17,1},{25,9},{2,18},{10... | collective-permute-start | bytes 786440 | tf_op jit(solution)/shard_map/ppermute | solution.py:157
  42.4 1.4 %collective-permute-start.23 = (bf16[4,16,2048]{2,1,0:T(8,128)(2,1)S(1)}, bf16[4,16,2048]{2,1,0:T(8,128)(2,1)S(1)}, u32[]{:S(2)}, u32[]{:S(2)}) collective-permute-start(bf16[4,16,2048]{2,1,0:T(8,128)(2,1)S(1)} %get-tuple-element.52), channel_id=1, source_target_pairs={{0,24},{8,16},{16,8},{24,0},{1,25},{9,17},{17,9},{25,1},{2,26},{10... | collective-permute-start | bytes 786440 | tf_op jit(solution)/shard_map/ppermute | solution.py:157
  43.8 4.2 %collective-permute-done.19.refs_2_ = bf16[4,16,2048]{2,1,0:T(8,128)(2,1)S(1)} collective-permute-done((bf16[4,16,2048]{2,1,0:T(8,128)(2,1)S(1)}, bf16[4,16,2048]{2,1,0:T(8,128)(2,1)S(1)}, u32[]{:S(2)}, u32[]{:S(2)}) %collective-permute-start.19) | collective-permute-done | bytes 262176 | tf_op jit(solution)/shard_map/ppermute | solution.py:157
  48.1 4.6 %copy-done = bf16[1,4,2048,768]{3,2,1,0:T(8,128)(2,1)S(1)} copy-done((bf16[1,4,2048,768]{3,2,1,0:T(8,128)(2,1)S(1)}, bf16[1,4,2048,768]{3,2,1,0:T(8,128)(2,1)}, u32[]{:S(2)}) %copy-start) | copy-done | bytes 12582936
  52.6 4.6 %copy-done.2 = bf16[1,4,2048,768]{3,2,1,0:T(8,128)(2,1)S(1)} copy-done((bf16[1,4,2048,768]{3,2,1,0:T(8,128)(2,1)S(1)}, bf16[1,4,2048,768]{3,2,1,0:T(8,128)(2,1)}, u32[]{:S(2)}) %copy-start.2) | copy-done | bytes 12582936
  57.2 4.6 %copy-done.4 = bf16[1,4,768,2048]{3,2,1,0:T(8,128)(2,1)S(1)} copy-done((bf16[1,4,768,2048]{3,2,1,0:T(8,128)(2,1)S(1)}, bf16[1,4,768,2048]{3,2,1,0:T(8,128)(2,1)}, u32[]{:S(2)}) %copy-start.4) | copy-done | bytes 12582936
  61.8 7.1 %forward.1 = (f32[4,64,768]{2,1,0:T(8,128)S(1)}, f32[4,64,768]{2,1,0:T(8,128)S(1)}, bf16[4,64,768]{2,1,0:T(8,128)(2,1)S(1)}, bf16[4,16,2048]{2,1,0:T(8,128)(2,1)...) custom-call(bf16[4,16,2048]{2,1,0:T(8,128)(2,1)S(1)} %get-tuple-element.5, ...), custom_call_target="tpu_custom_call" | custom-call | flops 9663676416 | bytes 37748736 | tf_op jit(solution)/shard_map/forward/pallas_call | solution.py:362
  68.9 1.6 %collective-permute-start.24 = (bf16[4,16,2048]{2,1,0:T(8,128)(2,1)S(1)}, bf16[4,16,2048]{2,1,0:T(8,128)(2,1)S(1)}, u32[]{:S(2)}, u32[]{:S(2)}) collective-permute-start(bf16[4,16,2048]{2,1,0:T(8,128)(2,1)S(1)} %get-tuple-element.65), channel_id=1, source_target_pairs={{0,8},{8,0},{16,24},{24,16},{1,9},{9,1},{17,25},{25,17},{2,10},{10... | collective-permute-start | bytes 786440 | tf_op jit(solution)/shard_map/ppermute | solution.py:157
  70.5 2.5 %collective-permute-start.25 = (bf16[4,16,2048]{2,1,0:T(8,128)(2,1)S(1)}, bf16[4,16,2048]{2,1,0:T(8,128)(2,1)S(1)}, u32[]{:S(2)}, u32[]{:S(2)}) collective-permute-start(bf16[4,16,2048]{2,1,0:T(8,128)(2,1)S(1)} %get-tuple-element.66), channel_id=1, source_target_pairs={{0,16},{8,24},{16,0},{24,8},{1,17},{9,25},{17,1},{25,9},{2,18},{10... | collective-permute-start | bytes 786440 | tf_op jit(solution)/shard_map/ppermute | solution.py:157
  73.0 4.6 %copy-done.3 = bf16[1,4,2048,768]{3,2,1,0:T(8,128)(2,1)S(1)} copy-done((bf16[1,4,2048,768]{3,2,1,0:T(8,128)(2,1)S(1)}, bf16[1,4,2048,768]{3,2,1,0:T(8,128)(2,1)}, u32[]{:S(2)}) %copy-start.3) | copy-done | bytes 12582936
  77.6 4.6 %copy-done.5 = bf16[1,4,768,2048]{3,2,1,0:T(8,128)(2,1)S(1)} copy-done((bf16[1,4,768,2048]{3,2,1,0:T(8,128)(2,1)S(1)}, bf16[1,4,768,2048]{3,2,1,0:T(8,128)(2,1)}, u32[]{:S(2)}) %copy-start.5) | copy-done | bytes 12582936
  82.2 13.5 %backward.1 = (bf16[4,64,768]{2,1,0:T(8,128)(2,1)S(1)}, bf16[4,64,768]{2,1,0:T(8,128)(2,1)S(1)}, bf16[4,16,2048]{2,1,0:T(8,128)(2,1)S(1)}, bf16[4,16,2048]{2,1,0...) custom-call(bf16[4,16,2048]{2,1,0:T(8,128)(2,1)S(1)} %get-tuple-element.49.refs_0_, ...), custom_call_target="tpu_custom_call" | custom-call | flops 9663676416 | bytes 37748736 | tf_op jit(solution)/shard_map/backward/pallas_call | solution.py:373
  95.7 0.7 combine_out.1
  96.5 1.5 %collective-permute-start.31 = (bf16[4,16,2048]{2,1,0:T(8,128)(2,1)S(1)}, bf16[4,16,2048]{2,1,0:T(8,128)(2,1)S(1)}, u32[]{:S(2)}, u32[]{:S(2)}) collective-permute-start(bf16[4,16,2048]{2,1,0:T(8,128)(2,1)S(1)} %get-tuple-element.61), channel_id=1, source_target_pairs={{0,8},{8,0},{16,24},{24,16},{1,9},{9,1},{17,25},{25,17},{2,10},{10... | collective-permute-start | bytes 786440 | tf_op jit(solution)/shard_map/ppermute | solution.py:157
  98.0 2.0 %collective-permute-start.32 = (bf16[4,16,2048]{2,1,0:T(8,128)(2,1)S(1)}, bf16[4,16,2048]{2,1,0:T(8,128)(2,1)S(1)}, u32[]{:S(2)}, u32[]{:S(2)}) collective-permute-start(bf16[4,16,2048]{2,1,0:T(8,128)(2,1)S(1)} %get-tuple-element.62), channel_id=1, source_target_pairs={{0,16},{8,24},{16,0},{24,8},{1,17},{9,25},{17,1},{25,9},{2,18},{10... | collective-permute-start | bytes 786440 | tf_op jit(solution)/shard_map/ppermute | solution.py:157
  100.0 0.1 fusion.6
  100.1 3.6 %collective-permute-start.28 = (bf16[32,2048]{1,0:T(8,128)(2,1)S(1)}, bf16[32,2048]{1,0:T(8,128)(2,1)S(1)}, u32[]{:S(2)}, u32[]{:S(2)}) collective-permute-start(bf16[32,2048]{1,0:T(8,128)(2,1)S(1)} %get-tuple-element.84), channel_id=1, source_target_pairs={{0,2},{1,3},{2,0},{3,1},{4,6},{5,7},{6,4},{7,5},{8,10},{9,11},{10,... | collective-permute-start | bytes 393224 | tf_op jit(solution)/shard_map/ppermute | solution.py:157
  103.7 0.5 collective-permute-start.30
  104.3 1.4 %collective-permute-done.31.refs_2_ = bf16[4,16,2048]{2,1,0:T(8,128)(2,1)S(1)} collective-permute-done((bf16[4,16,2048]{2,1,0:T(8,128)(2,1)S(1)}, bf16[4,16,2048]{2,1,0:T(8,128)(2,1)S(1)}, u32[]{:S(2)}, u32[]{:S(2)}) %collective-permute-start.31) | collective-permute-done | bytes 262176 | tf_op jit(solution)/shard_map/ppermute | solution.py:157
  105.6 2.6 %collective-permute-start.29 = (bf16[32,2048]{1,0:T(8,128)(2,1)S(1)}, bf16[32,2048]{1,0:T(8,128)(2,1)S(1)}, u32[]{:S(2)}, u32[]{:S(2)}) collective-permute-start(bf16[32,2048]{1,0:T(8,128)(2,1)S(1)} %get-tuple-element.86), channel_id=1, source_target_pairs={{0,4},{1,5},{2,6},{3,7},{4,0},{5,1},{6,2},{7,3},{8,12},{9,13},{10,... | collective-permute-start | bytes 393224 | tf_op jit(solution)/shard_map/ppermute | solution.py:157
  108.3 6.4 %down_grads.1 = bf16[1,4,768,2048]{3,2,1,0:T(8,128)(2,1)} custom-call(bf16[4,16,2048]{2,1,0:T(8,128)(2,1)S(1)} %get-tuple-element.49.refs_0_, bf16[4,16,2048]{2,1,0:T(8,128)(2,1)S(1)} %collective-permute-done.21.refs_1_, bf16[4,16,2048]{2,1,0:T(8,128)(2,1)S(1)} %collective-permute-done.22.refs_2_, bf16[4,16,2048]{2,1,0:T(8,128)(2,1)S(1)} %collective-permute-done.23.refs_3_, ...), custom_call_target="tpu_custom_call" | custom-call | flops 3221225472 | bytes 12582912 | tf_op jit(solution)/shard_map/down_grads/pallas_call | solution.py:412
  114.6 0.4 combine_dx.1
  115.2 1.8 %collective-permute-done.29 = bf16[32,2048]{1,0:T(8,128)(2,1)S(1)} collective-permute-done((bf16[32,2048]{1,0:T(8,128)(2,1)S(1)}, bf16[32,2048]{1,0:T(8,128)(2,1)S(1)}, u32[]{:S(2)}, u32[]{:S(2)}) %collective-permute-start.29) | collective-permute-done | bytes 131104 | tf_op jit(solution)/shard_map/ppermute | solution.py:157
  117.0 0.7 fusion.5
  117.7 0.1 fusion.9
  117.8 0.6 collective-permute-start.35
  118.4 2.2 %collective-permute-start.37 = (bf16[32,2048]{1,0:T(8,128)(2,1)S(1)}, bf16[32,2048]{1,0:T(8,128)(2,1)S(1)}, u32[]{:S(2)}, u32[]{:S(2)}) collective-permute-start(bf16[32,2048]{1,0:T(8,128)(2,1)S(1)} %get-tuple-element.82), channel_id=1, source_target_pairs={{0,6},{1,7},{2,4},{3,5},{4,2},{5,3},{6,0},{7,1},{8,14},{9,15},{10,... | collective-permute-start | bytes 393224 | tf_op jit(solution)/shard_map/ppermute | solution.py:157
  120.6 0.8 collective-permute-start.36
  121.4 9.9 %up_grads.1 = (bf16[1,4,2048,768]{3,2,1,0:T(8,128)(2,1)}, bf16[1,4,2048,768]{3,2,1,0:T(8,128)(2,1)}) custom-call(bf16[4,16,2048]{2,1,0:T(8,128)(2,1)S(1)} %get-tuple-element.53.refs_0_, bf16[4,16,2048]{2,1,0:T(8,128)(2,1)S(1)} %collective-permute-done.18.refs_1_, bf16[4,16,2048]{2,1,0:T(8,128)(2,1)S(1)} %collective-permute-done.19.refs_2_, ...), custom_call_target="tpu_custom_call" | custom-call | flops 6442450944 | bytes 25165824 | tf_op jit(solution)/shard_map/up_grads/pallas_call | solution.py:425
  131.2 1.8 %collective-permute-done.36 = bf16[32,2048]{1,0:T(8,128)(2,1)S(1)} collective-permute-done((bf16[32,2048]{1,0:T(8,128)(2,1)S(1)}, bf16[32,2048]{1,0:T(8,128)(2,1)S(1)}, u32[]{:S(2)}, u32[]{:S(2)}) %collective-permute-start.36) | collective-permute-done | bytes 131104 | tf_op jit(solution)/shard_map/ppermute | solution.py:157
  133.0 0.7 fusion.2
  (50 shorter events, 0.4 us)
Async XLA Ops:
  0.6 11.5 %collective-permute-start.3 = (bf16[32,2048]{1,0:T(8,128)(2,1)}, bf16[32,2048]{1,0:T(8,128)(2,1)S(1)}, u32[]{:S(2)}, u32[]{:S(2)}) collective-permute-start(bf16[32,2048]{1,0:T(8,128)(2,1)} %refs_0_.1), channel_id=1, source_target_pairs={{0,4},{1,5},{2,6},{3,7},{4,0},{5,1},{6,2},{7,3},{8,12},{9,13},{10,... | collective-permute-start | bytes 393224 | tf_op jit(solution)/shard_map/ppermute | solution.py:157
  7.1 15.7 %collective-permute-start.9 = (f32[32,128]{1,0:T(8,128)S(1)}, f32[32,128]{1,0:T(8,128)S(1)}, u32[]{:S(2)}, u32[]{:S(2)}) collective-permute-start(f32[32,128]{1,0:T(8,128)S(1)} %maximum_maximum_fusion.refs_8_), channel_id=1, source_target_pairs={{0,6},{1,7},{2,4},{3,5},{4,2},{5,3},{6,0},{7,1},{8,14},{9,15},{10,... | collective-permute-start | bytes 49160 | tf_op jit(solution)/shard_map/ppermute | solution.py:157
  8.5 14.4 %collective-permute-start.8 = (f32[32,128]{1,0:T(8,128)S(1)}, f32[32,128]{1,0:T(8,128)S(1)}, u32[]{:S(2)}, u32[]{:S(2)}) collective-permute-start(f32[32,128]{1,0:T(8,128)S(1)} %maximum_maximum_fusion.refs_8_), channel_id=1, source_target_pairs={{0,4},{1,5},{2,6},{3,7},{4,0},{5,1},{6,2},{7,3},{8,12},{9,13},{10,... | collective-permute-start | bytes 49160 | tf_op jit(solution)/shard_map/ppermute | solution.py:157
  10.1 13.2 %collective-permute-start.7 = (f32[32,128]{1,0:T(8,128)S(1)}, f32[32,128]{1,0:T(8,128)S(1)}, u32[]{:S(2)}, u32[]{:S(2)}) collective-permute-start(f32[32,128]{1,0:T(8,128)S(1)} %maximum_maximum_fusion.refs_8_), channel_id=1, source_target_pairs={{0,2},{1,3},{2,0},{3,1},{4,6},{5,7},{6,4},{7,5},{8,10},{9,11},{10,... | collective-permute-start | bytes 49160 | tf_op jit(solution)/shard_map/ppermute | solution.py:157
  11.5 8.0 %collective-permute-start.1 = (bf16[32,2048]{1,0:T(8,128)(2,1)}, bf16[32,2048]{1,0:T(8,128)(2,1)S(1)}, u32[]{:S(2)}, u32[]{:S(2)}) collective-permute-start(bf16[32,2048]{1,0:T(8,128)(2,1)} %refs_0_.1), channel_id=1, source_target_pairs={{0,2},{1,3},{2,0},{3,1},{4,6},{5,7},{6,4},{7,5},{8,10},{9,11},{10,... | collective-permute-start | bytes 393224 | tf_op jit(solution)/shard_map/ppermute | solution.py:157
  12.2 7.3 %collective-permute-start.5 = (bf16[32,2048]{1,0:T(8,128)(2,1)}, bf16[32,2048]{1,0:T(8,128)(2,1)S(1)}, u32[]{:S(2)}, u32[]{:S(2)}) collective-permute-start(bf16[32,2048]{1,0:T(8,128)(2,1)} %refs_0_.1), channel_id=1, source_target_pairs={{0,6},{1,7},{2,4},{3,5},{4,2},{5,3},{6,0},{7,1},{8,14},{9,15},{10,... | collective-permute-start | bytes 393224 | tf_op jit(solution)/shard_map/ppermute | solution.py:157
  19.5 5.4 %collective-permute-start = (bf16[32,2048]{1,0:T(8,128)(2,1)}, bf16[32,2048]{1,0:T(8,128)(2,1)S(1)}, u32[]{:S(2)}, u32[]{:S(2)}) collective-permute-start(bf16[32,2048]{1,0:T(8,128)(2,1)} %refs_0_.1), channel_id=1, source_target_pairs={{0,1},{1,0},{2,3},{3,2},{4,5},{5,4},{6,7},{7,6},{8,9},{9,8},{10,11... | collective-permute-start | bytes 393224 | tf_op jit(solution)/shard_map/ppermute | solution.py:157
  19.5 8.3 %collective-permute-start.16 = (bf16[32,2048]{1,0:T(8,128)(2,1)}, bf16[32,2048]{1,0:T(8,128)(2,1)S(1)}, u32[]{:S(2)}, u32[]{:S(2)}) collective-permute-start(bf16[32,2048]{1,0:T(8,128)(2,1)} %refs_0_.2), channel_id=1, source_target_pairs={{0,6},{1,7},{2,4},{3,5},{4,2},{5,3},{6,0},{7,1},{8,14},{9,15},{10,... | collective-permute-start | bytes 393224 | tf_op jit(solution)/shard_map/ppermute | solution.py:157
  22.8 2.2 %collective-permute-start.4 = (bf16[32,2048]{1,0:T(8,128)(2,1)S(1)}, bf16[32,2048]{1,0:T(8,128)(2,1)S(1)}, u32[]{:S(2)}, u32[]{:S(2)}) collective-permute-start(bf16[32,2048]{1,0:T(8,128)(2,1)S(1)} %collective-permute-done.3.refs_4_), channel_id=1, source_target_pairs={{0,1},{1,0},{2,3},{3,2},{4,5},{5,4},{6,7},{7,6},{8,9},{9,8},{10,11... | collective-permute-start | bytes 393224 | tf_op jit(solution)/shard_map/ppermute | solution.py:157
  22.9 3.1 %collective-permute-start.2 = (bf16[32,2048]{1,0:T(8,128)(2,1)S(1)}, bf16[32,2048]{1,0:T(8,128)(2,1)S(1)}, u32[]{:S(2)}, u32[]{:S(2)}) collective-permute-start(bf16[32,2048]{1,0:T(8,128)(2,1)S(1)} %collective-permute-done.1.refs_2_), channel_id=1, source_target_pairs={{0,1},{1,0},{2,3},{3,2},{4,5},{5,4},{6,7},{7,6},{8,9},{9,8},{10,11... | collective-permute-start | bytes 393224 | tf_op jit(solution)/shard_map/ppermute | solution.py:157
  23.4 1.3 collective-permute-start.10
  24.7 3.2 %collective-permute-start.6 = (bf16[32,2048]{1,0:T(8,128)(2,1)S(1)}, bf16[32,2048]{1,0:T(8,128)(2,1)S(1)}, u32[]{:S(2)}, u32[]{:S(2)}) collective-permute-start(bf16[32,2048]{1,0:T(8,128)(2,1)S(1)} %collective-permute-done.5.refs_6_), channel_id=1, source_target_pairs={{0,1},{1,0},{2,3},{3,2},{4,5},{5,4},{6,7},{7,6},{8,9},{9,8},{10,11... | collective-permute-start | bytes 393224 | tf_op jit(solution)/shard_map/ppermute | solution.py:157
  24.9 9.6 %collective-permute-start.14 = (bf16[32,2048]{1,0:T(8,128)(2,1)}, bf16[32,2048]{1,0:T(8,128)(2,1)S(1)}, u32[]{:S(2)}, u32[]{:S(2)}) collective-permute-start(bf16[32,2048]{1,0:T(8,128)(2,1)} %refs_0_.2), channel_id=1, source_target_pairs={{0,4},{1,5},{2,6},{3,7},{4,0},{5,1},{6,2},{7,3},{8,12},{9,13},{10,... | collective-permute-start | bytes 393224 | tf_op jit(solution)/shard_map/ppermute | solution.py:157
  25.1 10.9 %collective-permute-start.12 = (bf16[32,2048]{1,0:T(8,128)(2,1)}, bf16[32,2048]{1,0:T(8,128)(2,1)S(1)}, u32[]{:S(2)}, u32[]{:S(2)}) collective-permute-start(bf16[32,2048]{1,0:T(8,128)(2,1)} %refs_0_.2), channel_id=1, source_target_pairs={{0,2},{1,3},{2,0},{3,1},{4,6},{5,7},{6,4},{7,5},{8,10},{9,11},{10,... | collective-permute-start | bytes 393224 | tf_op jit(solution)/shard_map/ppermute | solution.py:157
  26.0 11.4 %collective-permute-start.11 = (bf16[32,2048]{1,0:T(8,128)(2,1)}, bf16[32,2048]{1,0:T(8,128)(2,1)S(1)}, u32[]{:S(2)}, u32[]{:S(2)}) collective-permute-start(bf16[32,2048]{1,0:T(8,128)(2,1)} %refs_0_.2), channel_id=1, source_target_pairs={{0,1},{1,0},{2,3},{3,2},{4,5},{5,4},{6,7},{7,6},{8,9},{9,8},{10,11... | collective-permute-start | bytes 393224 | tf_op jit(solution)/shard_map/ppermute | solution.py:157
  27.8 9.6 %collective-permute-start.17 = (bf16[32,2048]{1,0:T(8,128)(2,1)S(1)}, bf16[32,2048]{1,0:T(8,128)(2,1)S(1)}, u32[]{:S(2)}, u32[]{:S(2)}) collective-permute-start(bf16[32,2048]{1,0:T(8,128)(2,1)S(1)} %collective-permute-done.16.refs_6_), channel_id=1, source_target_pairs={{0,1},{1,0},{2,3},{3,2},{4,5},{5,4},{6,7},{7,6},{8,9},{9,8},{10,11... | collective-permute-start | bytes 393224 | tf_op jit(solution)/shard_map/ppermute | solution.py:157
  27.9 0.9 copy-start.6
  30.6 11.8 %collective-permute-start.18 = (bf16[4,16,2048]{2,1,0:T(8,128)(2,1)S(1)}, bf16[4,16,2048]{2,1,0:T(8,128)(2,1)S(1)}, u32[]{:S(2)}, u32[]{:S(2)}) collective-permute-start(bf16[4,16,2048]{2,1,0:T(8,128)(2,1)S(1)} %get-tuple-element.54), channel_id=1, source_target_pairs={{0,8},{8,0},{16,24},{24,16},{1,9},{9,1},{17,25},{25,17},{2,10},{10... | collective-permute-start | bytes 786440 | tf_op jit(solution)/shard_map/ppermute | solution.py:157
  34.4 13.6 %collective-permute-start.19 = (bf16[4,16,2048]{2,1,0:T(8,128)(2,1)S(1)}, bf16[4,16,2048]{2,1,0:T(8,128)(2,1)S(1)}, u32[]{:S(2)}, u32[]{:S(2)}) collective-permute-start(bf16[4,16,2048]{2,1,0:T(8,128)(2,1)S(1)} %get-tuple-element.55), channel_id=1, source_target_pairs={{0,16},{8,24},{16,0},{24,8},{1,17},{9,25},{17,1},{25,9},{2,18},{10... | collective-permute-start | bytes 786440 | tf_op jit(solution)/shard_map/ppermute | solution.py:157
  36.0 12.1 %collective-permute-start.20 = (bf16[4,16,2048]{2,1,0:T(8,128)(2,1)S(1)}, bf16[4,16,2048]{2,1,0:T(8,128)(2,1)S(1)}, u32[]{:S(2)}, u32[]{:S(2)}) collective-permute-start(bf16[4,16,2048]{2,1,0:T(8,128)(2,1)S(1)} %get-tuple-element.56), channel_id=1, source_target_pairs={{0,24},{8,16},{16,8},{24,0},{1,25},{9,17},{17,9},{25,1},{2,26},{10... | collective-permute-start | bytes 786440 | tf_op jit(solution)/shard_map/ppermute | solution.py:157
  37.4 1.3 %collective-permute-start.15 = (bf16[32,2048]{1,0:T(8,128)(2,1)S(1)}, bf16[32,2048]{1,0:T(8,128)(2,1)S(1)}, u32[]{:S(2)}, u32[]{:S(2)}) collective-permute-start(bf16[32,2048]{1,0:T(8,128)(2,1)S(1)} %collective-permute-done.14.refs_4_), channel_id=1, source_target_pairs={{0,1},{1,0},{2,3},{3,2},{4,5},{5,4},{6,7},{7,6},{8,9},{9,8},{10,11... | collective-permute-start | bytes 393224 | tf_op jit(solution)/shard_map/ppermute | solution.py:157
  37.4 1.5 %collective-permute-start.13 = (bf16[32,2048]{1,0:T(8,128)(2,1)S(1)}, bf16[32,2048]{1,0:T(8,128)(2,1)S(1)}, u32[]{:S(2)}, u32[]{:S(2)}) collective-permute-start(bf16[32,2048]{1,0:T(8,128)(2,1)S(1)} %collective-permute-done.12.refs_2_), channel_id=1, source_target_pairs={{0,1},{1,0},{2,3},{3,2},{4,5},{5,4},{6,7},{7,6},{8,9},{9,8},{10,11... | collective-permute-start | bytes 393224 | tf_op jit(solution)/shard_map/ppermute | solution.py:157
  38.9 0.9 copy-start.7
  40.3 32.7 %collective-permute-start.21 = (bf16[4,16,2048]{2,1,0:T(8,128)(2,1)S(1)}, bf16[4,16,2048]{2,1,0:T(8,128)(2,1)S(1)}, u32[]{:S(2)}, u32[]{:S(2)}) collective-permute-start(bf16[4,16,2048]{2,1,0:T(8,128)(2,1)S(1)} %get-tuple-element.50), channel_id=1, source_target_pairs={{0,8},{8,0},{16,24},{24,16},{1,9},{9,1},{17,25},{25,17},{2,10},{10... | collective-permute-start | bytes 786440 | tf_op jit(solution)/shard_map/ppermute | solution.py:157
  40.9 32.1 %collective-permute-start.22 = (bf16[4,16,2048]{2,1,0:T(8,128)(2,1)S(1)}, bf16[4,16,2048]{2,1,0:T(8,128)(2,1)S(1)}, u32[]{:S(2)}, u32[]{:S(2)}) collective-permute-start(bf16[4,16,2048]{2,1,0:T(8,128)(2,1)S(1)} %get-tuple-element.51), channel_id=1, source_target_pairs={{0,16},{8,24},{16,0},{24,8},{1,17},{9,25},{17,1},{25,9},{2,18},{10... | collective-permute-start | bytes 786440 | tf_op jit(solution)/shard_map/ppermute | solution.py:157
  42.4 30.6 %collective-permute-start.23 = (bf16[4,16,2048]{2,1,0:T(8,128)(2,1)S(1)}, bf16[4,16,2048]{2,1,0:T(8,128)(2,1)S(1)}, u32[]{:S(2)}, u32[]{:S(2)}) collective-permute-start(bf16[4,16,2048]{2,1,0:T(8,128)(2,1)S(1)} %get-tuple-element.52), channel_id=1, source_target_pairs={{0,24},{8,16},{16,8},{24,0},{1,25},{9,17},{17,9},{25,1},{2,26},{10... | collective-permute-start | bytes 786440 | tf_op jit(solution)/shard_map/ppermute | solution.py:157
  48.1 4.6 %copy-start = (bf16[1,4,2048,768]{3,2,1,0:T(8,128)(2,1)S(1)}, bf16[1,4,2048,768]{3,2,1,0:T(8,128)(2,1)}, u32[]{:S(2)}) copy-start(bf16[1,4,2048,768]{3,2,1,0:T(8,128)(2,1)} %refs_6_.3) | copy-start | bytes 37748740
  52.6 4.6 %copy-start.2 = (bf16[1,4,2048,768]{3,2,1,0:T(8,128)(2,1)S(1)}, bf16[1,4,2048,768]{3,2,1,0:T(8,128)(2,1)}, u32[]{:S(2)}) copy-start(bf16[1,4,2048,768]{3,2,1,0:T(8,128)(2,1)} %refs_7_.1) | copy-start | bytes 37748740
  57.2 4.6 %copy-start.4 = (bf16[1,4,768,2048]{3,2,1,0:T(8,128)(2,1)S(1)}, bf16[1,4,768,2048]{3,2,1,0:T(8,128)(2,1)}, u32[]{:S(2)}) copy-start(bf16[1,4,768,2048]{3,2,1,0:T(8,128)(2,1)} %refs_8_.1) | copy-start | bytes 37748740
  61.8 11.2 %copy-start.1 = (bf16[1,4,2048,768]{3,2,1,0:T(8,128)(2,1)S(1)}, bf16[1,4,2048,768]{3,2,1,0:T(8,128)(2,1)}, u32[]{:S(2)}) copy-start(bf16[1,4,2048,768]{3,2,1,0:T(8,128)(2,1)} %refs_6_.3) | copy-start | bytes 37748740
  68.9 26.7 %collective-permute-start.24 = (bf16[4,16,2048]{2,1,0:T(8,128)(2,1)S(1)}, bf16[4,16,2048]{2,1,0:T(8,128)(2,1)S(1)}, u32[]{:S(2)}, u32[]{:S(2)}) collective-permute-start(bf16[4,16,2048]{2,1,0:T(8,128)(2,1)S(1)} %get-tuple-element.65), channel_id=1, source_target_pairs={{0,8},{8,0},{16,24},{24,16},{1,9},{9,1},{17,25},{25,17},{2,10},{10... | collective-permute-start | bytes 786440 | tf_op jit(solution)/shard_map/ppermute | solution.py:157
  70.5 25.2 %collective-permute-start.25 = (bf16[4,16,2048]{2,1,0:T(8,128)(2,1)S(1)}, bf16[4,16,2048]{2,1,0:T(8,128)(2,1)S(1)}, u32[]{:S(2)}, u32[]{:S(2)}) collective-permute-start(bf16[4,16,2048]{2,1,0:T(8,128)(2,1)S(1)} %get-tuple-element.66), channel_id=1, source_target_pairs={{0,16},{8,24},{16,0},{24,8},{1,17},{9,25},{17,1},{25,9},{2,18},{10... | collective-permute-start | bytes 786440 | tf_op jit(solution)/shard_map/ppermute | solution.py:157
  73.0 22.7 %collective-permute-start.26 = (bf16[4,16,2048]{2,1,0:T(8,128)(2,1)S(1)}, bf16[4,16,2048]{2,1,0:T(8,128)(2,1)S(1)}, u32[]{:S(2)}, u32[]{:S(2)}) collective-permute-start(bf16[4,16,2048]{2,1,0:T(8,128)(2,1)S(1)} %get-tuple-element.67), channel_id=1, source_target_pairs={{0,24},{8,16},{16,8},{24,0},{1,25},{9,17},{17,9},{25,1},{2,26},{10... | collective-permute-start | bytes 786440 | tf_op jit(solution)/shard_map/ppermute | solution.py:157
  73.0 4.6 %copy-start.3 = (bf16[1,4,2048,768]{3,2,1,0:T(8,128)(2,1)S(1)}, bf16[1,4,2048,768]{3,2,1,0:T(8,128)(2,1)}, u32[]{:S(2)}) copy-start(bf16[1,4,2048,768]{3,2,1,0:T(8,128)(2,1)} %refs_7_.1) | copy-start | bytes 37748740
  77.6 4.6 %copy-start.5 = (bf16[1,4,768,2048]{3,2,1,0:T(8,128)(2,1)S(1)}, bf16[1,4,768,2048]{3,2,1,0:T(8,128)(2,1)}, u32[]{:S(2)}) copy-start(bf16[1,4,768,2048]{3,2,1,0:T(8,128)(2,1)} %refs_8_.1) | copy-start | bytes 37748740
  96.4 3.6 %collective-permute-start.27 = (bf16[4,32,2048]{2,1,0:T(8,128)(2,1)S(1)}, bf16[4,32,2048]{2,1,0:T(8,128)(2,1)S(1)}, u32[]{:S(2)}, u32[]{:S(2)}) collective-permute-start(bf16[4,32,2048]{2,1,0:T(8,128)(2,1)S(1)} %get-tuple-element.69), channel_id=1, source_target_pairs={{0,1},{1,0},{2,3},{3,2},{4,5},{5,4},{6,7},{7,6},{8,9},{9,8},{10,11... | collective-permute-start | bytes 1572872 | tf_op jit(solution)/shard_map/ppermute | solution.py:157
  96.5 9.2 %collective-permute-start.31 = (bf16[4,16,2048]{2,1,0:T(8,128)(2,1)S(1)}, bf16[4,16,2048]{2,1,0:T(8,128)(2,1)S(1)}, u32[]{:S(2)}, u32[]{:S(2)}) collective-permute-start(bf16[4,16,2048]{2,1,0:T(8,128)(2,1)S(1)} %get-tuple-element.61), channel_id=1, source_target_pairs={{0,8},{8,0},{16,24},{24,16},{1,9},{9,1},{17,25},{25,17},{2,10},{10... | collective-permute-start | bytes 786440 | tf_op jit(solution)/shard_map/ppermute | solution.py:157
  98.0 16.7 %collective-permute-start.32 = (bf16[4,16,2048]{2,1,0:T(8,128)(2,1)S(1)}, bf16[4,16,2048]{2,1,0:T(8,128)(2,1)S(1)}, u32[]{:S(2)}, u32[]{:S(2)}) collective-permute-start(bf16[4,16,2048]{2,1,0:T(8,128)(2,1)S(1)} %get-tuple-element.62), channel_id=1, source_target_pairs={{0,16},{8,24},{16,0},{24,8},{1,17},{9,25},{17,1},{25,9},{2,18},{10... | collective-permute-start | bytes 786440 | tf_op jit(solution)/shard_map/ppermute | solution.py:157
  100.0 14.6 %collective-permute-start.33 = (bf16[4,16,2048]{2,1,0:T(8,128)(2,1)S(1)}, bf16[4,16,2048]{2,1,0:T(8,128)(2,1)S(1)}, u32[]{:S(2)}, u32[]{:S(2)}) collective-permute-start(bf16[4,16,2048]{2,1,0:T(8,128)(2,1)S(1)} %get-tuple-element.63), channel_id=1, source_target_pairs={{0,24},{8,16},{16,8},{24,0},{1,25},{9,17},{17,9},{25,1},{2,26},{10... | collective-permute-start | bytes 786440 | tf_op jit(solution)/shard_map/ppermute | solution.py:157
  100.1 15.0 %collective-permute-start.28 = (bf16[32,2048]{1,0:T(8,128)(2,1)S(1)}, bf16[32,2048]{1,0:T(8,128)(2,1)S(1)}, u32[]{:S(2)}, u32[]{:S(2)}) collective-permute-start(bf16[32,2048]{1,0:T(8,128)(2,1)S(1)} %get-tuple-element.84), channel_id=1, source_target_pairs={{0,2},{1,3},{2,0},{3,1},{4,6},{5,7},{6,4},{7,5},{8,10},{9,11},{10,... | collective-permute-start | bytes 393224 | tf_op jit(solution)/shard_map/ppermute | solution.py:157
  103.7 11.4 %collective-permute-start.30 = (bf16[32,2048]{1,0:T(8,128)(2,1)S(1)}, bf16[32,2048]{1,0:T(8,128)(2,1)S(1)}, u32[]{:S(2)}, u32[]{:S(2)}) collective-permute-start(bf16[32,2048]{1,0:T(8,128)(2,1)S(1)} %get-tuple-element.85), channel_id=1, source_target_pairs={{0,6},{1,7},{2,4},{3,5},{4,2},{5,3},{6,0},{7,1},{8,14},{9,15},{10,... | collective-permute-start | bytes 393224 | tf_op jit(solution)/shard_map/ppermute | solution.py:157
  105.6 11.3 %collective-permute-start.29 = (bf16[32,2048]{1,0:T(8,128)(2,1)S(1)}, bf16[32,2048]{1,0:T(8,128)(2,1)S(1)}, u32[]{:S(2)}, u32[]{:S(2)}) collective-permute-start(bf16[32,2048]{1,0:T(8,128)(2,1)S(1)} %get-tuple-element.86), channel_id=1, source_target_pairs={{0,4},{1,5},{2,6},{3,7},{4,0},{5,1},{6,2},{7,3},{8,12},{9,13},{10,... | collective-permute-start | bytes 393224 | tf_op jit(solution)/shard_map/ppermute | solution.py:157
  115.1 2.6 %collective-permute-start.34 = (bf16[4,32,2048]{2,1,0:T(8,128)(2,1)S(1)}, bf16[4,32,2048]{2,1,0:T(8,128)(2,1)S(1)}, u32[]{:S(2)}, u32[]{:S(2)}) collective-permute-start(bf16[4,32,2048]{2,1,0:T(8,128)(2,1)S(1)} %get-tuple-element.75), channel_id=1, source_target_pairs={{0,1},{1,0},{2,3},{3,2},{4,5},{5,4},{6,7},{7,6},{8,9},{9,8},{10,11... | collective-permute-start | bytes 1572872 | tf_op jit(solution)/shard_map/ppermute | solution.py:157
  117.8 13.4 %collective-permute-start.35 = (bf16[32,2048]{1,0:T(8,128)(2,1)S(1)}, bf16[32,2048]{1,0:T(8,128)(2,1)S(1)}, u32[]{:S(2)}, u32[]{:S(2)}) collective-permute-start(bf16[32,2048]{1,0:T(8,128)(2,1)S(1)} %get-tuple-element.81), channel_id=1, source_target_pairs={{0,2},{1,3},{2,0},{3,1},{4,6},{5,7},{6,4},{7,5},{8,10},{9,11},{10,... | collective-permute-start | bytes 393224 | tf_op jit(solution)/shard_map/ppermute | solution.py:157
  118.4 12.8 %collective-permute-start.37 = (bf16[32,2048]{1,0:T(8,128)(2,1)S(1)}, bf16[32,2048]{1,0:T(8,128)(2,1)S(1)}, u32[]{:S(2)}, u32[]{:S(2)}) collective-permute-start(bf16[32,2048]{1,0:T(8,128)(2,1)S(1)} %get-tuple-element.82), channel_id=1, source_target_pairs={{0,6},{1,7},{2,4},{3,5},{4,2},{5,3},{6,0},{7,1},{8,14},{9,15},{10,... | collective-permute-start | bytes 393224 | tf_op jit(solution)/shard_map/ppermute | solution.py:157
  120.6 12.4 %collective-permute-start.36 = (bf16[32,2048]{1,0:T(8,128)(2,1)S(1)}, bf16[32,2048]{1,0:T(8,128)(2,1)S(1)}, u32[]{:S(2)}, u32[]{:S(2)}) collective-permute-start(bf16[32,2048]{1,0:T(8,128)(2,1)S(1)} %get-tuple-element.83), channel_id=1, source_target_pairs={{0,4},{1,5},{2,6},{3,7},{4,0},{5,1},{6,2},{7,3},{8,12},{9,13},{10,... | collective-permute-start | bytes 393224 | tf_op jit(solution)/shard_map/ppermute | solution.py:157

commit v2 on v1

--- a/solution.py
+++ b/solution.py
@@ -11,6 +11,7 @@
 EXPERTS = 128
 TOPK = 8
 RGROUPS = 8
+GLIMIT = 4
 CAP = 2
 
 
@@ -161,62 +162,70 @@
     return pl.BlockSpec(memory_space=pltpu.VMEM)
 
 
-def select_tokens_kernel(local, count, width, place_ref, *refs):
+def pack_kernel(tokens_ref, upstream_ref, choice_ref, pick_ref, weight_ref, packed_ref):
+    count, width = tokens_ref.shape
+    per_group = EXPERTS // RGROUPS
+    parts = []
+    for k in range(TOPK):
+        group, place = choice_ref[k // 2 : k // 2 + 1, :], pick_ref[k // 2, k % 2 : k % 2 + 1, :]
+        parts.append((group * per_group + place).astype(jnp.float32))
+    left = weight_ref[...]
+    for _ in range(3):
+        high = left.astype(jnp.bfloat16).astype(jnp.float32)
+        parts.append(high)
+        left = left - high
+    parts.append(jnp.zeros((TABLE - 4 * TOPK, count), jnp.float32))
+    packed_ref[:, :width] = tokens_ref[...]
+    packed_ref[:, width : 2 * width] = upstream_ref[...]
+    packed_ref[:, 2 * width :] = jnp.concatenate(parts, axis=0).T.astype(jnp.bfloat16)
+
+
+def select_kernel(local, count, place_ref, *refs):
     pieces, rest = refs[:PLACES], refs[PLACES:]
-    near, rest = rest[: PLACES // 2], rest[PLACES // 2 :]
-    far, rest = rest[0], rest[1:]
-    outs, (pick_ref, pick_t_ref, high_ref, low_ref, scale_ref), full = rest[:COLUMNS], rest[COLUMNS:-1], rest[-1]
+    x_outs, dy_outs, rest = rest[:COLUMNS], rest[COLUMNS : 2 * COLUMNS], rest[2 * COLUMNS :]
+    pick_t_ref, high_ref, low_ref, full = rest
+    width = full.shape[1] // 2
     total = PLACES * count
     rows = COLUMNS * local * PLACES * CAP
-    tables = []
     for j in range(PLACES):
-        full[j * count : (j + 1) * count, :] = pieces[j][...]
-        tables.append(far[j // 2] if j % 2 else near[j // 2][...])
-    table = jnp.concatenate(tables, axis=0)
-    row = lax.broadcasted_iota(jnp.int32, (1, rows), 1)
+        full[j * count : (j + 1) * count, :] = pieces[j][:, : full.shape[1]]
+    table = jnp.concatenate([piece[:, full.shape[1] :].astype(jnp.float32) for piece in pieces], axis=0).T
+    row = lax.broadcasted_iota(jnp.int32, (rows, 1), 0)
     slot = row % CAP
     piece = row // CAP % PLACES
     column = place_ref[0] ^ (row // (CAP * PLACES * local))
     expert = (column * PLACES + place_ref[1]) * local + row // (CAP * PLACES) % local
     expert = expert.astype(jnp.float32)
-    member = jnp.zeros((total, rows), jnp.float32)
-    weight = jnp.zeros((total, rows), jnp.float32)
+    member = jnp.zeros((rows, total), jnp.float32)
+    weight = jnp.zeros((rows, total), jnp.float32)
     for k in range(TOPK):
-        same = table[:, k : k + 1] == expert
-        value = table[:, TOPK + k : TOPK + k + 1]
+        same = table[k : k + 1, :] == expert
         member = jnp.where(same, 1.0, member)
+        value = table[TOPK + k : TOPK + k + 1, :] + table[2 * TOPK + k : 2 * TOPK + k + 1, :]
+        value = value + table[3 * TOPK + k : 3 * TOPK + k + 1, :]
         weight = jnp.where(same, value, weight)
-    token = lax.broadcasted_iota(jnp.int32, (total, 1), 0)
-    other = lax.broadcasted_iota(jnp.int32, (1, total), 1)
+    other = lax.broadcasted_iota(jnp.int32, (total, 1), 0)
+    token = lax.broadcasted_iota(jnp.int32, (1, total), 1)
     earlier = ((other < token) & (other // count == token // count)).astype(jnp.float32)
     rank = jnp.dot(
-        earlier.astype(jnp.bfloat16), member.astype(jnp.bfloat16), preferred_element_type=jnp.float32
+        member.astype(jnp.bfloat16), earlier.astype(jnp.bfloat16), preferred_element_type=jnp.float32
     )
     kept = (member > 0.5) & (rank == slot.astype(jnp.float32)) & (token // count == piece)
-    pick_t = jnp.where(kept, 1.0, 0.0)
+    pick = jnp.where(kept, 1.0, 0.0)
     weight = jnp.where(kept, weight, 0.0)
+    scale = jnp.sum(weight, axis=1, keepdims=True)
+    chosen = jnp.dot(pick.astype(jnp.bfloat16), full[...], preferred_element_type=jnp.float32)
+    x_rows = chosen[:, :width].astype(jnp.bfloat16)
+    dy_rows = (chosen[:, width:] * scale).astype(jnp.bfloat16)
+    part = rows // COLUMNS
+    for m in range(COLUMNS):
+        x_outs[m][...] = x_rows[m * part : (m + 1) * part].reshape(x_outs[m].shape)
+        dy_outs[m][...] = dy_rows[m * part : (m + 1) * part].reshape(dy_outs[m].shape)
+    pick_t_ref[...] = pick.T.astype(jnp.bfloat16)
+    weight = weight.T
     high = weight.astype(jnp.bfloat16)
-    pick = pick_t.T.astype(jnp.bfloat16)
-    pick_ref[...] = pick
-    pick_t_ref[...] = pick_t.astype(jnp.bfloat16)
     high_ref[...] = high
     low_ref[...] = (weight - high.astype(jnp.float32)).astype(jnp.bfloat16)
-    scale_ref[...] = jnp.sum(weight.T, axis=1, keepdims=True)
-    chosen = jnp.dot(pick, full[...], preferred_element_type=jnp.float32).astype(jnp.bfloat16)
-    part = rows // COLUMNS
-    for m in range(COLUMNS):
-        outs[m][...] = chosen[m * part : (m + 1) * part].reshape(outs[m].shape)
-
-
-def select_upstream_kernel(count, pick_ref, scale_ref, *refs):
-    pieces, outs, full = refs[:PLACES], refs[PLACES:-1], refs[-1]
-    for j in range(PLACES):
-        full[j * count : (j + 1) * count, :] = pieces[j][...]
-    chosen = jnp.dot(pick_ref[...], full[...], preferred_element_type=jnp.float32)
-    chosen = (chosen * scale_ref[...]).astype(jnp.bfloat16)
-    part = chosen.shape[0] // COLUMNS
-    for m in range(COLUMNS):
-        outs[m][...] = chosen[m * part : (m + 1) * part].reshape(outs[m].shape)
 
 
 def combine_kernel(count, terms, *refs):
@@ -246,6 +255,12 @@
     return jnp.concatenate([piece[e] for piece in pieces], axis=0)
 
 
+def load_kernel(source_ref, held_ref, done):
+    copy = pltpu.make_async_copy(source_ref, held_ref, done)
+    copy.start()
+    copy.wait()
+
+
 def forward_kernel(*refs):
     pieces = refs[:COLUMNS]
     wg_ref, wu_ref, wd_ref, g_ref, u_ref, h_ref = refs[COLUMNS : COLUMNS + 6]
@@ -307,12 +322,17 @@
 def on_device(tokens, upstream, gate_weights, group_choice, pair_pick, w_gate, w_up, w_down):
     count, width = tokens.shape
     local, hidden = w_gate.shape[1], w_gate.shape[3]
+    if COLUMNS * PLACES * local != EXPERTS or local * PLACES * CAP != 2 * count:
+        return on_device_general(
+            tokens, upstream, gate_weights, group_choice, pair_pick, w_gate, w_up, w_down
+        )
     rows = COLUMNS * local * PLACES * CAP
     part = PLACES * CAP
     bf16, f32 = jnp.bfloat16, jnp.float32
 
     def along(value):
-        return [value] + [swap(value, "inner", PLACES, 2 * z) for z in (1, 2, 3)]
+        far = [swap(value, "inner", PLACES, 2 * z) for z in (2, 3, 1)]
+        return [value, far[2], far[0], far[1]]
 
     def both(near):
         return [one for z in near for one in (z, swap(z, "inner", PLACES, 1))]
@@ -320,40 +340,61 @@
     def exchange(pieces):
         return [pieces[0]] + [swap(pieces[m], "group", COLUMNS, m) for m in (1, 2, 3)]
 
-    ids = expert_ids(group_choice, pair_pick)
-    blank = jnp.zeros((count, TABLE - 2 * TOPK), f32)
-    table = jnp.concatenate([ids.astype(f32), gate_weights, blank], axis=1)
-    x_near = along(tokens)
-    table_near = along(table)
-    table_far = swap(jnp.stack(table_near), "inner", PLACES, 1)
+    def loaded(weight, name):
+        return pl.pallas_call(
+            load_kernel,
+            name=name,
+            out_shape=pltpu.VMEM(weight.shape, bf16),
+            in_specs=[pl.BlockSpec(memory_space=pltpu.HBM)],
+            out_specs=whole(),
+            scratch_shapes=[pltpu.SemaphoreType.DMA],
+            compiler_params=params(8),
+            cost_estimate=cost(0, 2 * weight.size * 2),
+        )(pltpu.with_memory_space_constraint(weight, pltpu.HBM))
+
+    full_width = 2 * width + TABLE
+    own = pl.pallas_call(
+        pack_kernel,
+        name="pack",
+        grid=(1,),
+        out_shape=jax.ShapeDtypeStruct((count, full_width), bf16),
+        in_specs=[
+            pl.BlockSpec((count, width), lambda n: (0, 0)),
+            pl.BlockSpec((count, width), lambda n: (0, 0)),
+            pl.BlockSpec((GLIMIT, count), lambda n: (0, 0)),
+            pl.BlockSpec((GLIMIT, TOPK // GLIMIT, count), lambda n: (0, 0, 0)),
+            pl.BlockSpec((TOPK, count), lambda n: (0, 0)),
+        ],
+        out_specs=pl.BlockSpec((count, full_width), lambda n: (0, 0)),
+        compiler_params=params(8, 1),
+    )(
+        *(
+            pltpu.with_memory_space_constraint(value, pltpu.HBM)
+            for value in (tokens, upstream, group_choice.T, pair_pick.transpose(1, 2, 0), gate_weights.T)
+        )
+    )
+    near = along(own)
+    held_gate = loaded(w_gate, "load_gate")
+    held_up = loaded(w_up, "load_up")
+    held_down = loaded(w_down, "load_down")
+    *far, held_gate, held_up = lax.optimization_barrier((*near[2:], held_gate, held_up))
+    near = near[:2] + far
 
     sent = [jax.ShapeDtypeStruct((local, part, width), bf16)] * COLUMNS
     square = jax.ShapeDtypeStruct((rows, rows), bf16)
     place = jnp.stack([lax.axis_index("group"), lax.axis_index("inner")]).astype(jnp.int32)
-    *x_send, pick, pick_t, high, low, scale = pl.pallas_call(
-        functools.partial(select_tokens_kernel, local, count, width),
-        name="select_tokens",
-        out_shape=sent + [square] * 4 + [jax.ShapeDtypeStruct((rows, 1), f32)],
-        in_specs=[pl.BlockSpec(memory_space=pltpu.SMEM)] + [whole()] * (PLACES + PLACES // 2 + 1),
-        out_specs=[whole()] * (COLUMNS + 5),
-        scratch_shapes=[pltpu.VMEM((PLACES * count, width), bf16)],
-        compiler_params=params(8),
-        cost_estimate=cost(2 * rows * rows * width, 4 * rows * width),
-    )(place, *both(x_near), *table_near, table_far)
-    x_recv = exchange(x_send)
-
-    dy_near = along(after(upstream, *x_near[1:]))
-    dy_send = pl.pallas_call(
-        functools.partial(select_upstream_kernel, count),
-        name="select_upstream",
-        out_shape=sent,
-        in_specs=[whole()] * (PLACES + 2),
-        out_specs=[whole()] * COLUMNS,
-        scratch_shapes=[pltpu.VMEM((PLACES * count, width), bf16)],
-        compiler_params=params(8),
-        cost_estimate=cost(2 * rows * rows * width, 4 * rows * width),
-    )(pick, scale, *both(dy_near))
-    dy_recv = exchange(dy_send)
+    *sends, pick_t, high, low = pl.pallas_call(
+        functools.partial(select_kernel, local, count),
+        name="select",
+        out_shape=sent + sent + [square] * 3,
+        in_specs=[pl.BlockSpec(memory_space=pltpu.SMEM)] + [whole()] * PLACES,
+        out_specs=[whole()] * (2 * COLUMNS + 3),
+        scratch_shapes=[pltpu.VMEM((PLACES * count, 2 * width), bf16)],
+        compiler_params=params(16),
+        cost_estimate=cost(4 * rows * rows * width, 8 * rows * width),
+    )(place, *both(near))
+    x_recv = exchange(sends[:COLUMNS])
+    dy_recv = exchange(sends[COLUMNS:])
 
     hid = lambda t: jax.ShapeDtypeStruct((local, rows // local, hidden), t)
     weight_bytes = 2 * local * width * hidden
@@ -367,7 +408,7 @@
         out_specs=[whole()] * (COLUMNS + 3),
         compiler_params=params(8),
         cost_estimate=cost(12 * flops, 3 * weight_bytes),
-    )(after(x_recv[0], *dy_send), *x_recv[1:], w_gate, w_up, w_down)
+    )(*x_recv, held_gate, held_up, held_down)
     out_back = exchange(out_send)
 
     dg, du, *dx_send = pl.pallas_call(
@@ -378,7 +419,7 @@
         out_specs=[whole()] * (COLUMNS + 2),
         compiler_params=params(8),
         cost_estimate=cost(12 * flops, 3 * weight_bytes),
-    )(*dy_recv, g, u, w_gate, w_up, w_down)
+    )(*dy_recv, g, u, held_gate, held_up, held_down)
     dx_back = exchange(dx_send)
 
     def combine(blends, pieces, name):

time: 134 us -> 111 us (0.83)
  starting transfers between devices: 44.3 us -> 26.9 us
  local copies, waits for them, and re-layouts: 25.6 us -> 9.56 us
  Pallas kernels: 40.2 us -> 54.6 us
  waiting for transfers between devices: 19.5 us -> 16.8 us
  other arithmetic: 3.28 us -> 1.75 us
    ppermute x38 -> x27, starting transfers between devices: 44.3 us -> 26.9 us  [swap(): return lax.ppermute(value, axis, [(k, k ^ mask) for k in range(size)])]
    unnamed x17 -> x12, local copies, waits for them, and re-layouts: 25.4 us -> 9.56 us
    pallas_call x2 -> x5, Pallas kernels: 2.25 us -> 16.7 us  [the longest x3 14 us: loaded(): pl.pallas_call(load_kernel, name=name, out_shape=pltpu.VMEM(weight.shape,...]
    ppermute x38 -> x27, waiting for transfers between devices: 19.5 us -> 16.8 us  [swap(): return lax.ppermute(value, axis, [(k, k ^ mask) for k in range(size)])]
  transfers between devices with their start and end apart: 38 -> 27, of which waited for: 10 -> 10; matrix products, arithmetic and copies ran while one was open for 3% -> 1% of each run, Pallas kernels for 30% -> 46%
where the time goes in v2:
time: 111 us
  Pallas kernels  54.6 us (49%)
  starting transfers between devices  26.9 us (24%)
  waiting for transfers between devices  16.8 us (15%)
  local copies, waits for them, and re-layouts  9.56 us (9%)
  other arithmetic  1.75 us (2%)
    ppermute x27, starting transfers between devices, swap(): return lax.ppermute(value, axis, [(k, k ^ mask) for k in range(size)])  26.9 us
    ppermute x27, waiting for transfers between devices, swap(): return lax.ppermute(value, axis, [(k, k ^ mask) for k in range(size)])  16.8 us
    pallas_call x3, Pallas kernels, loaded(): pl.pallas_call(load_kernel, name=name, out_shape=pltpu.VMEM(weight.shape,...  14 us
    pallas_call x1, Pallas kernels, on_device(): pl.pallas_call(backward_kernel, name='backward', out_shape=[hid(bf16), hi...  13.5 us
    pallas_call x1, Pallas kernels, on_device(): pl.pallas_call(up_grads_kernel, name='up_grads', grid=(local,), out_shape...  9.85 us
    unnamed x12, local copies, waits for them, and re-layouts  9.56 us
    pallas_call x1, Pallas kernels, on_device(): pl.pallas_call(forward_kernel, name='forward', out_shape=[hid(f32), hid(f...  7.14 us
    pallas_call x1, Pallas kernels, on_device(): pl.pallas_call(down_grads_kernel, name='down_grads', grid=(local,), out_s...  6.37 us
  transfers between devices with their start and end apart: 27, of which 10 were waited for; matrix products, arithmetic and copies ran while one was open for 1% of the time, Pallas kernels for 46%

profile of v2, /device:TPU:0, one launch (start us, length us, event | category | flops | bytes accessed | tf_op | source)
XLA Modules:
  0.0 110.5 jit_solution(3587884058539942133)
XLA Ops:
  0.6 1.1 pack.1.refs_0_
  1.7 5.1 %collective-permute-start.4 = (bf16[32,4224]{1,0:T(8,128)(2,1)S(1)}, bf16[32,4224]{1,0:T(8,128)(2,1)S(1)}, u32[]{:S(2)}, u32[]{:S(2)}) collective-permute-start(bf16[32,4224]{1,0:T(8,128)(2,1)S(1)} %pack.1.refs_0_), channel_id=1, source_target_pairs={{0,6},{1,7},{2,4},{3,5},{4,2},{5,3},{6,0},{7,1},{8,14},{9,15},{10,... | collective-permute-start | bytes 811016 | tf_op jit(solution)/shard_map/ppermute | solution.py:158
  6.8 0.0 collective-permute-start.3
  6.8 0.6 collective-permute-start.1
  7.4 0.0 collective-permute-start
  7.4 4.6 %load_gate.1.refs_4_.refs_6_ = bf16[1,4,2048,768]{3,2,1,0:T(8,128)(2,1)S(1)} custom-call(bf16[1,4,2048,768]{3,2,1,0:T(8,128)(2,1)} %source_ref.3), custom_call_target="tpu_custom_call" | custom-call | bytes 25165824 | tf_op jit(solution)/shard_map/load_gate/pallas_call | solution.py:344
  12.0 0.0 copy-start
  12.0 4.8 %copy-done = bf16[1,4,2048,768]{3,2,1,0:T(8,128)(2,1)} copy-done((bf16[1,4,2048,768]{3,2,1,0:T(8,128)(2,1)}, bf16[1,4,2048,768]{3,2,1,0:T(8,128)(2,1)S(1)}, u32[]{:S(2)}) %copy-start) | copy-done | bytes 12582936
  16.8 4.6 %load_up.1.refs_5_.refs_7_ = bf16[1,4,2048,768]{3,2,1,0:T(8,128)(2,1)S(1)} custom-call(bf16[1,4,2048,768]{3,2,1,0:T(8,128)(2,1)} %source_ref.4), custom_call_target="tpu_custom_call" | custom-call | bytes 25165824 | tf_op jit(solution)/shard_map/load_up/pallas_call | solution.py:344
  21.4 0.0 copy-start.1
  21.4 4.8 %copy-done.1 = bf16[1,4,2048,768]{3,2,1,0:T(8,128)(2,1)} copy-done((bf16[1,4,2048,768]{3,2,1,0:T(8,128)(2,1)}, bf16[1,4,2048,768]{3,2,1,0:T(8,128)(2,1)S(1)}, u32[]{:S(2)}) %copy-start.1) | copy-done | bytes 12582936
  26.2 3.6 %collective-permute-done.3.refs_4_ = bf16[32,4224]{1,0:T(8,128)(2,1)S(1)} collective-permute-done((bf16[32,4224]{1,0:T(8,128)(2,1)S(1)}, bf16[32,4224]{1,0:T(8,128)(2,1)S(1)}, u32[]{:S(2)}, u32[]{:S(2)}) %collective-permute-start.3) | collective-permute-done | bytes 270368 | tf_op jit(solution)/shard_map/ppermute | solution.py:158
  29.8 0.0 collective-permute-start.5
  29.8 0.0 collective-permute-done.1.refs_2_
  29.8 0.5 collective-permute-start.2
  30.3 0.0 collective-permute-start.6
  30.3 0.1 pad_add_fusion.place_ref
  30.4 0.0 collective-permute-done.refs_1_
  30.4 1.3 %collective-permute-done.2.refs_3_ = bf16[32,4224]{1,0:T(8,128)(2,1)S(1)} collective-permute-done((bf16[32,4224]{1,0:T(8,128)(2,1)S(1)}, bf16[32,4224]{1,0:T(8,128)(2,1)S(1)}, u32[]{:S(2)}, u32[]{:S(2)}) %collective-permute-start.2) | collective-permute-done | bytes 270368 | tf_op jit(solution)/shard_map/ppermute | solution.py:158
  31.7 0.0 collective-permute-done.5.refs_5_
  31.7 0.4 collective-permute-done.6.refs_7_
  32.1 1.6 %select.1 = (bf16[4,16,2048]{2,1,0:T(8,128)(2,1)S(1)}, bf16[4,16,2048]{2,1,0:T(8,128)(2,1)S(1)}, bf16[4,16,2048]{2,1,0:T(8,128)(2,1)S(1)}, bf16[4,16,2048]{2,1,0...) custom-call(s32[2]{0:T(128)S(1)} %pad_add_fusion.place_ref, ...), custom_call_target="tpu_custom_call" | custom-call | flops 536870912 | bytes 4194304 | tf_op jit(solution)/shard_map/select/pallas_call | solution.py:386
  33.7 1.6 %collective-permute-start.7 = (bf16[4,16,2048]{2,1,0:T(8,128)(2,1)S(1)}, bf16[4,16,2048]{2,1,0:T(8,128)(2,1)S(1)}, u32[]{:S(2)}, u32[]{:S(2)}) collective-permute-start(bf16[4,16,2048]{2,1,0:T(8,128)(2,1)S(1)} %get-tuple-element.48), channel_id=1, source_target_pairs={{0,8},{8,0},{16,24},{24,16},{1,9},{9,1},{17,25},{25,17},{2,10},{10... | collective-permute-start | bytes 786440 | tf_op jit(solution)/shard_map/ppermute | solution.py:158
  35.3 1.5 %collective-permute-start.8 = (bf16[4,16,2048]{2,1,0:T(8,128)(2,1)S(1)}, bf16[4,16,2048]{2,1,0:T(8,128)(2,1)S(1)}, u32[]{:S(2)}, u32[]{:S(2)}) collective-permute-start(bf16[4,16,2048]{2,1,0:T(8,128)(2,1)S(1)} %get-tuple-element.49), channel_id=1, source_target_pairs={{0,16},{8,24},{16,0},{24,8},{1,17},{9,25},{17,1},{25,9},{2,18},{10... | collective-permute-start | bytes 786440 | tf_op jit(solution)/shard_map/ppermute | solution.py:158
  36.8 0.5 collective-permute-start.9
  37.3 4.9 %load_down.1.refs_6_.refs_8_ = bf16[1,4,768,2048]{3,2,1,0:T(8,128)(2,1)S(1)} custom-call(bf16[1,4,768,2048]{3,2,1,0:T(8,128)(2,1)} %source_ref.5), custom_call_target="tpu_custom_call" | custom-call | bytes 25165824 | tf_op jit(solution)/shard_map/load_down/pallas_call | solution.py:344
  42.2 2.0 %collective-permute-start.10 = (bf16[4,16,2048]{2,1,0:T(8,128)(2,1)S(1)}, bf16[4,16,2048]{2,1,0:T(8,128)(2,1)S(1)}, u32[]{:S(2)}, u32[]{:S(2)}) collective-permute-start(bf16[4,16,2048]{2,1,0:T(8,128)(2,1)S(1)} %get-tuple-element.55), channel_id=1, source_target_pairs={{0,8},{8,0},{16,24},{24,16},{1,9},{9,1},{17,25},{25,17},{2,10},{10... | collective-permute-start | bytes 786440 | tf_op jit(solution)/shard_map/ppermute | solution.py:158
  44.2 1.6 %collective-permute-start.11 = (bf16[4,16,2048]{2,1,0:T(8,128)(2,1)S(1)}, bf16[4,16,2048]{2,1,0:T(8,128)(2,1)S(1)}, u32[]{:S(2)}, u32[]{:S(2)}) collective-permute-start(bf16[4,16,2048]{2,1,0:T(8,128)(2,1)S(1)} %get-tuple-element.56), channel_id=1, source_target_pairs={{0,16},{8,24},{16,0},{24,8},{1,17},{9,25},{17,1},{25,9},{2,18},{10... | collective-permute-start | bytes 786440 | tf_op jit(solution)/shard_map/ppermute | solution.py:158
  45.8 3.3 %collective-permute-done.8.refs_2_ = bf16[4,16,2048]{2,1,0:T(8,128)(2,1)S(1)} collective-permute-done((bf16[4,16,2048]{2,1,0:T(8,128)(2,1)S(1)}, bf16[4,16,2048]{2,1,0:T(8,128)(2,1)S(1)}, u32[]{:S(2)}, u32[]{:S(2)}) %collective-permute-start.8) | collective-permute-done | bytes 262176 | tf_op jit(solution)/shard_map/ppermute | solution.py:158
  49.1 0.4 collective-permute-done.9.refs_3_
  49.6 7.1 %forward.1 = (f32[4,64,768]{2,1,0:T(8,128)S(1)}, f32[4,64,768]{2,1,0:T(8,128)S(1)}, bf16[4,64,768]{2,1,0:T(8,128)(2,1)S(1)}, bf16[4,16,2048]{2,1,0:T(8,128)(2,1)...) custom-call(bf16[4,16,2048]{2,1,0:T(8,128)(2,1)S(1)} %get-tuple-element.4, ...), custom_call_target="tpu_custom_call" | custom-call | flops 9663676416 | bytes 37748736 | tf_op jit(solution)/shard_map/forward/pallas_call | solution.py:403
  56.7 1.6 %collective-permute-start.13 = (bf16[4,16,2048]{2,1,0:T(8,128)(2,1)S(1)}, bf16[4,16,2048]{2,1,0:T(8,128)(2,1)S(1)}, u32[]{:S(2)}, u32[]{:S(2)}) collective-permute-start(bf16[4,16,2048]{2,1,0:T(8,128)(2,1)S(1)} %get-tuple-element.65), channel_id=1, source_target_pairs={{0,8},{8,0},{16,24},{24,16},{1,9},{9,1},{17,25},{25,17},{2,10},{10... | collective-permute-start | bytes 786440 | tf_op jit(solution)/shard_map/ppermute | solution.py:158
  58.3 0.6 collective-permute-start.14
  58.9 0.0 collective-permute-done.10.refs_1_
  58.9 1.4 %collective-permute-start.15 = (bf16[4,16,2048]{2,1,0:T(8,128)(2,1)S(1)}, bf16[4,16,2048]{2,1,0:T(8,128)(2,1)S(1)}, u32[]{:S(2)}, u32[]{:S(2)}) collective-permute-start(bf16[4,16,2048]{2,1,0:T(8,128)(2,1)S(1)} %get-tuple-element.67), channel_id=1, source_target_pairs={{0,24},{8,16},{16,8},{24,0},{1,25},{9,17},{17,9},{25,1},{2,26},{10... | collective-permute-start | bytes 786440 | tf_op jit(solution)/shard_map/ppermute | solution.py:158
  60.3 0.0 collective-permute-done.11.refs_2_
  60.3 0.5 collective-permute-done.12.refs_3_
  60.8 13.5 %backward.1 = (bf16[4,64,768]{2,1,0:T(8,128)(2,1)S(1)}, bf16[4,64,768]{2,1,0:T(8,128)(2,1)S(1)}, bf16[4,16,2048]{2,1,0:T(8,128)(2,1)S(1)}, bf16[4,16,2048]{2,1,0...) custom-call(bf16[4,16,2048]{2,1,0:T(8,128)(2,1)S(1)} %get-tuple-element.54.refs_0_, ...), custom_call_target="tpu_custom_call" | custom-call | flops 9663676416 | bytes 37748736 | tf_op jit(solution)/shard_map/backward/pallas_call | solution.py:414
  74.3 0.0 collective-permute-done.14.refs_4_
  74.3 0.0 collective-permute-done.15.refs_5_
  74.3 0.7 combine_out.1
  75.0 0.1 collective-permute-start.16
  75.1 1.5 %collective-permute-start.20 = (bf16[4,16,2048]{2,1,0:T(8,128)(2,1)S(1)}, bf16[4,16,2048]{2,1,0:T(8,128)(2,1)S(1)}, u32[]{:S(2)}, u32[]{:S(2)}) collective-permute-start(bf16[4,16,2048]{2,1,0:T(8,128)(2,1)S(1)} %get-tuple-element.61), channel_id=1, source_target_pairs={{0,8},{8,0},{16,24},{24,16},{1,9},{9,1},{17,25},{25,17},{2,10},{10... | collective-permute-start | bytes 786440 | tf_op jit(solution)/shard_map/ppermute | solution.py:158
  76.6 0.6 collective-permute-start.21
  77.2 1.5 %collective-permute-start.22 = (bf16[4,16,2048]{2,1,0:T(8,128)(2,1)S(1)}, bf16[4,16,2048]{2,1,0:T(8,128)(2,1)S(1)}, u32[]{:S(2)}, u32[]{:S(2)}) collective-permute-start(bf16[4,16,2048]{2,1,0:T(8,128)(2,1)S(1)} %get-tuple-element.63), channel_id=1, source_target_pairs={{0,24},{8,16},{16,8},{24,0},{1,25},{9,17},{17,9},{25,1},{2,26},{10... | collective-permute-start | bytes 786440 | tf_op jit(solution)/shard_map/ppermute | solution.py:158
  78.7 0.1 fusion.6
  78.8 0.1 collective-permute-start.17
  78.9 2.5 %collective-permute-start.19 = (bf16[32,2048]{1,0:T(8,128)(2,1)S(1)}, bf16[32,2048]{1,0:T(8,128)(2,1)S(1)}, u32[]{:S(2)}, u32[]{:S(2)}) collective-permute-start(bf16[32,2048]{1,0:T(8,128)(2,1)S(1)} %get-tuple-element.85), channel_id=1, source_target_pairs={{0,6},{1,7},{2,4},{3,5},{4,2},{5,3},{6,0},{7,1},{8,14},{9,15},{10,... | collective-permute-start | bytes 393224 | tf_op jit(solution)/shard_map/ppermute | solution.py:158
  81.4 2.9 %collective-permute-done.20.refs_2_ = bf16[4,16,2048]{2,1,0:T(8,128)(2,1)S(1)} collective-permute-done((bf16[4,16,2048]{2,1,0:T(8,128)(2,1)S(1)}, bf16[4,16,2048]{2,1,0:T(8,128)(2,1)S(1)}, u32[]{:S(2)}, u32[]{:S(2)}) %collective-permute-start.20) | collective-permute-done | bytes 262176 | tf_op jit(solution)/shard_map/ppermute | solution.py:158
  84.3 0.0 collective-permute-start.18
  84.3 6.4 %down_grads.1 = bf16[1,4,768,2048]{3,2,1,0:T(8,128)(2,1)} custom-call(bf16[4,16,2048]{2,1,0:T(8,128)(2,1)S(1)} %get-tuple-element.54.refs_0_, bf16[4,16,2048]{2,1,0:T(8,128)(2,1)S(1)} %collective-permute-done.10.refs_1_, bf16[4,16,2048]{2,1,0:T(8,128)(2,1)S(1)} %collective-permute-done.11.refs_2_, bf16[4,16,2048]{2,1,0:T(8,128)(2,1)S(1)} %collective-permute-done.12.refs_3_, ...), custom_call_target="tpu_custom_call" | custom-call | flops 3221225472 | bytes 12582912 | tf_op jit(solution)/shard_map/down_grads/pallas_call | solution.py:453
  90.7 0.2 collective-permute-done.22.refs_4_
  90.8 0.4 combine_dx.1
  91.3 0.1 collective-permute-start.23
  91.4 2.3 %collective-permute-done.18 = bf16[32,2048]{1,0:T(8,128)(2,1)S(1)} collective-permute-done((bf16[32,2048]{1,0:T(8,128)(2,1)S(1)}, bf16[32,2048]{1,0:T(8,128)(2,1)S(1)}, u32[]{:S(2)}, u32[]{:S(2)}) %collective-permute-start.18) | collective-permute-done | bytes 131104 | tf_op jit(solution)/shard_map/ppermute | solution.py:158
  93.7 0.7 fusion.5
  94.4 0.0 collective-permute-done.23
  94.4 0.1 fusion.9
  94.5 1.7 %collective-permute-start.24 = (bf16[32,2048]{1,0:T(8,128)(2,1)S(1)}, bf16[32,2048]{1,0:T(8,128)(2,1)S(1)}, u32[]{:S(2)}, u32[]{:S(2)}) collective-permute-start(bf16[32,2048]{1,0:T(8,128)(2,1)S(1)} %get-tuple-element.81), channel_id=1, source_target_pairs={{0,2},{1,3},{2,0},{3,1},{4,6},{5,7},{6,4},{7,5},{8,10},{9,11},{10,... | collective-permute-start | bytes 393224 | tf_op jit(solution)/shard_map/ppermute | solution.py:158
  96.3 1.4 %collective-permute-start.26 = (bf16[32,2048]{1,0:T(8,128)(2,1)S(1)}, bf16[32,2048]{1,0:T(8,128)(2,1)S(1)}, u32[]{:S(2)}, u32[]{:S(2)}) collective-permute-start(bf16[32,2048]{1,0:T(8,128)(2,1)S(1)} %get-tuple-element.82), channel_id=1, source_target_pairs={{0,6},{1,7},{2,4},{3,5},{4,2},{5,3},{6,0},{7,1},{8,14},{9,15},{10,... | collective-permute-start | bytes 393224 | tf_op jit(solution)/shard_map/ppermute | solution.py:158
  97.6 0.5 collective-permute-start.25
  98.1 9.9 %up_grads.1 = (bf16[1,4,2048,768]{3,2,1,0:T(8,128)(2,1)}, bf16[1,4,2048,768]{3,2,1,0:T(8,128)(2,1)}) custom-call(bf16[4,16,2048]{2,1,0:T(8,128)(2,1)S(1)} %get-tuple-element.47.refs_0_, bf16[4,16,2048]{2,1,0:T(8,128)(2,1)S(1)} %collective-permute-done.7.refs_1_, bf16[4,16,2048]{2,1,0:T(8,128)(2,1)S(1)} %collective-permute-done.8.refs_2_, ...), custom_call_target="tpu_custom_call" | custom-call | flops 6442450944 | bytes 25165824 | tf_op jit(solution)/shard_map/up_grads/pallas_call | solution.py:466
  108.0 1.8 %collective-permute-done.25 = bf16[32,2048]{1,0:T(8,128)(2,1)S(1)} collective-permute-done((bf16[32,2048]{1,0:T(8,128)(2,1)S(1)}, bf16[32,2048]{1,0:T(8,128)(2,1)S(1)}, u32[]{:S(2)}, u32[]{:S(2)}) %collective-permute-start.25) | collective-permute-done | bytes 131104 | tf_op jit(solution)/shard_map/ppermute | solution.py:158
  109.8 0.7 fusion.2
  (19 shorter events, 0.0 us)
Async XLA Ops:
  1.7 24.5 %collective-permute-start.4 = (bf16[32,4224]{1,0:T(8,128)(2,1)S(1)}, bf16[32,4224]{1,0:T(8,128)(2,1)S(1)}, u32[]{:S(2)}, u32[]{:S(2)}) collective-permute-start(bf16[32,4224]{1,0:T(8,128)(2,1)S(1)} %pack.1.refs_0_), channel_id=1, source_target_pairs={{0,6},{1,7},{2,4},{3,5},{4,2},{5,3},{6,0},{7,1},{8,14},{9,15},{10,... | collective-permute-start | bytes 811016 | tf_op jit(solution)/shard_map/ppermute | solution.py:158
  6.8 23.0 %collective-permute-start.3 = (bf16[32,4224]{1,0:T(8,128)(2,1)S(1)}, bf16[32,4224]{1,0:T(8,128)(2,1)S(1)}, u32[]{:S(2)}, u32[]{:S(2)}) collective-permute-start(bf16[32,4224]{1,0:T(8,128)(2,1)S(1)} %pack.1.refs_0_), channel_id=1, source_target_pairs={{0,4},{1,5},{2,6},{3,7},{4,0},{5,1},{6,2},{7,3},{8,12},{9,13},{10,... | collective-permute-start | bytes 811016 | tf_op jit(solution)/shard_map/ppermute | solution.py:158
  6.8 23.0 %collective-permute-start.1 = (bf16[32,4224]{1,0:T(8,128)(2,1)S(1)}, bf16[32,4224]{1,0:T(8,128)(2,1)S(1)}, u32[]{:S(2)}, u32[]{:S(2)}) collective-permute-start(bf16[32,4224]{1,0:T(8,128)(2,1)S(1)} %pack.1.refs_0_), channel_id=1, source_target_pairs={{0,2},{1,3},{2,0},{3,1},{4,6},{5,7},{6,4},{7,5},{8,10},{9,11},{10,... | collective-permute-start | bytes 811016 | tf_op jit(solution)/shard_map/ppermute | solution.py:158
  7.4 23.0 %collective-permute-start = (bf16[32,4224]{1,0:T(8,128)(2,1)S(1)}, bf16[32,4224]{1,0:T(8,128)(2,1)S(1)}, u32[]{:S(2)}, u32[]{:S(2)}) collective-permute-start(bf16[32,4224]{1,0:T(8,128)(2,1)S(1)} %pack.1.refs_0_), channel_id=1, source_target_pairs={{0,1},{1,0},{2,3},{3,2},{4,5},{5,4},{6,7},{7,6},{8,9},{9,8},{10,11... | collective-permute-start | bytes 811016 | tf_op jit(solution)/shard_map/ppermute | solution.py:158
  12.0 4.8 %copy-start = (bf16[1,4,2048,768]{3,2,1,0:T(8,128)(2,1)}, bf16[1,4,2048,768]{3,2,1,0:T(8,128)(2,1)S(1)}, u32[]{:S(2)}) copy-start(bf16[1,4,2048,768]{3,2,1,0:T(8,128)(2,1)S(1)} %load_gate.1.refs_4_.refs_6_) | copy-start | bytes 37748740
  21.4 4.8 %copy-start.1 = (bf16[1,4,2048,768]{3,2,1,0:T(8,128)(2,1)}, bf16[1,4,2048,768]{3,2,1,0:T(8,128)(2,1)S(1)}, u32[]{:S(2)}) copy-start(bf16[1,4,2048,768]{3,2,1,0:T(8,128)(2,1)S(1)} %load_up.1.refs_5_.refs_7_) | copy-start | bytes 37748740
  29.8 1.9 %collective-permute-start.5 = (bf16[32,4224]{1,0:T(8,128)(2,1)S(1)}, bf16[32,4224]{1,0:T(8,128)(2,1)S(1)}, u32[]{:S(2)}, u32[]{:S(2)}) collective-permute-start(bf16[32,4224]{1,0:T(8,128)(2,1)S(1)} %collective-permute-done.3.refs_4_), channel_id=1, source_target_pairs={{0,1},{1,0},{2,3},{3,2},{4,5},{5,4},{6,7},{7,6},{8,9},{9,8},{10,11... | collective-permute-start | bytes 811016 | tf_op jit(solution)/shard_map/ppermute | solution.py:158
  29.8 1.9 %collective-permute-start.2 = (bf16[32,4224]{1,0:T(8,128)(2,1)S(1)}, bf16[32,4224]{1,0:T(8,128)(2,1)S(1)}, u32[]{:S(2)}, u32[]{:S(2)}) collective-permute-start(bf16[32,4224]{1,0:T(8,128)(2,1)S(1)} %collective-permute-done.1.refs_2_), channel_id=1, source_target_pairs={{0,1},{1,0},{2,3},{3,2},{4,5},{5,4},{6,7},{7,6},{8,9},{9,8},{10,11... | collective-permute-start | bytes 811016 | tf_op jit(solution)/shard_map/ppermute | solution.py:158
  30.3 1.8 %collective-permute-start.6 = (bf16[32,4224]{1,0:T(8,128)(2,1)S(1)}, bf16[32,4224]{1,0:T(8,128)(2,1)S(1)}, u32[]{:S(2)}, u32[]{:S(2)}) collective-permute-start(bf16[32,4224]{1,0:T(8,128)(2,1)S(1)} %collective-permute-done.4.refs_6_), channel_id=1, source_target_pairs={{0,1},{1,0},{2,3},{3,2},{4,5},{5,4},{6,7},{7,6},{8,9},{9,8},{10,11... | collective-permute-start | bytes 811016 | tf_op jit(solution)/shard_map/ppermute | solution.py:158
  33.7 12.1 %collective-permute-start.7 = (bf16[4,16,2048]{2,1,0:T(8,128)(2,1)S(1)}, bf16[4,16,2048]{2,1,0:T(8,128)(2,1)S(1)}, u32[]{:S(2)}, u32[]{:S(2)}) collective-permute-start(bf16[4,16,2048]{2,1,0:T(8,128)(2,1)S(1)} %get-tuple-element.48), channel_id=1, source_target_pairs={{0,8},{8,0},{16,24},{24,16},{1,9},{9,1},{17,25},{25,17},{2,10},{10... | collective-permute-start | bytes 786440 | tf_op jit(solution)/shard_map/ppermute | solution.py:158
  35.3 13.8 %collective-permute-start.8 = (bf16[4,16,2048]{2,1,0:T(8,128)(2,1)S(1)}, bf16[4,16,2048]{2,1,0:T(8,128)(2,1)S(1)}, u32[]{:S(2)}, u32[]{:S(2)}) collective-permute-start(bf16[4,16,2048]{2,1,0:T(8,128)(2,1)S(1)} %get-tuple-element.49), channel_id=1, source_target_pairs={{0,16},{8,24},{16,0},{24,8},{1,17},{9,25},{17,1},{25,9},{2,18},{10... | collective-permute-start | bytes 786440 | tf_op jit(solution)/shard_map/ppermute | solution.py:158
  36.8 12.8 %slice-start = ((s8[12582912]{0:T(1024)(128)(4,1)}), s8[4194304]{0:T(1024)(128)(4,1)S(1)}, s32[]{:S(2)}) async-start(s8[12582912]{0:T(1024)(128)(4,1)} %bitcast.33), calls=%async_computation | async-start | bytes 8388608
  36.8 12.8 %slice-start.1 = ((s8[12582912]{0:T(1024)(128)(4,1)}), s8[4194304]{0:T(1024)(128)(4,1)S(1)}, s32[]{:S(2)}) async-start(s8[12582912]{0:T(1024)(128)(4,1)} %bitcast.33), calls=%async_computation.1 | async-start | bytes 8388608
  36.8 12.8 %slice-start.2 = ((s8[12582912]{0:T(1024)(128)(4,1)}), s8[4194304]{0:T(1024)(128)(4,1)S(1)}, s32[]{:S(2)}) async-start(s8[12582912]{0:T(1024)(128)(4,1)} %bitcast.33), calls=%async_computation.2 | async-start | bytes 8388608
  36.8 12.8 %copy-start.2 = (bf16[1,4,2048,768]{3,2,1,0:T(8,128)(2,1)S(1)}, bf16[1,4,2048,768]{3,2,1,0:T(8,128)(2,1)}, u32[]{:S(2)}) copy-start(bf16[1,4,2048,768]{3,2,1,0:T(8,128)(2,1)} %copy-done.1) | copy-start | bytes 37748740
  36.8 12.7 %collective-permute-start.9 = (bf16[4,16,2048]{2,1,0:T(8,128)(2,1)S(1)}, bf16[4,16,2048]{2,1,0:T(8,128)(2,1)S(1)}, u32[]{:S(2)}, u32[]{:S(2)}) collective-permute-start(bf16[4,16,2048]{2,1,0:T(8,128)(2,1)S(1)} %get-tuple-element.50), channel_id=1, source_target_pairs={{0,24},{8,16},{16,8},{24,0},{1,25},{9,17},{17,9},{25,1},{2,26},{10... | collective-permute-start | bytes 786440 | tf_op jit(solution)/shard_map/ppermute | solution.py:158
  42.2 16.7 %collective-permute-start.10 = (bf16[4,16,2048]{2,1,0:T(8,128)(2,1)S(1)}, bf16[4,16,2048]{2,1,0:T(8,128)(2,1)S(1)}, u32[]{:S(2)}, u32[]{:S(2)}) collective-permute-start(bf16[4,16,2048]{2,1,0:T(8,128)(2,1)S(1)} %get-tuple-element.55), channel_id=1, source_target_pairs={{0,8},{8,0},{16,24},{24,16},{1,9},{9,1},{17,25},{25,17},{2,10},{10... | collective-permute-start | bytes 786440 | tf_op jit(solution)/shard_map/ppermute | solution.py:158
  44.2 16.1 %collective-permute-start.11 = (bf16[4,16,2048]{2,1,0:T(8,128)(2,1)S(1)}, bf16[4,16,2048]{2,1,0:T(8,128)(2,1)S(1)}, u32[]{:S(2)}, u32[]{:S(2)}) collective-permute-start(bf16[4,16,2048]{2,1,0:T(8,128)(2,1)S(1)} %get-tuple-element.56), channel_id=1, source_target_pairs={{0,16},{8,24},{16,0},{24,8},{1,17},{9,25},{17,1},{25,9},{2,18},{10... | collective-permute-start | bytes 786440 | tf_op jit(solution)/shard_map/ppermute | solution.py:158
  45.8 15.0 %collective-permute-start.12 = (bf16[4,16,2048]{2,1,0:T(8,128)(2,1)S(1)}, bf16[4,16,2048]{2,1,0:T(8,128)(2,1)S(1)}, u32[]{:S(2)}, u32[]{:S(2)}) collective-permute-start(bf16[4,16,2048]{2,1,0:T(8,128)(2,1)S(1)} %get-tuple-element.57), channel_id=1, source_target_pairs={{0,24},{8,16},{16,8},{24,0},{1,25},{9,17},{17,9},{25,1},{2,26},{10... | collective-permute-start | bytes 786440 | tf_op jit(solution)/shard_map/ppermute | solution.py:158
  56.7 17.6 %collective-permute-start.13 = (bf16[4,16,2048]{2,1,0:T(8,128)(2,1)S(1)}, bf16[4,16,2048]{2,1,0:T(8,128)(2,1)S(1)}, u32[]{:S(2)}, u32[]{:S(2)}) collective-permute-start(bf16[4,16,2048]{2,1,0:T(8,128)(2,1)S(1)} %get-tuple-element.65), channel_id=1, source_target_pairs={{0,8},{8,0},{16,24},{24,16},{1,9},{9,1},{17,25},{25,17},{2,10},{10... | collective-permute-start | bytes 786440 | tf_op jit(solution)/shard_map/ppermute | solution.py:158
  58.3 16.0 %collective-permute-start.14 = (bf16[4,16,2048]{2,1,0:T(8,128)(2,1)S(1)}, bf16[4,16,2048]{2,1,0:T(8,128)(2,1)S(1)}, u32[]{:S(2)}, u32[]{:S(2)}) collective-permute-start(bf16[4,16,2048]{2,1,0:T(8,128)(2,1)S(1)} %get-tuple-element.66), channel_id=1, source_target_pairs={{0,16},{8,24},{16,0},{24,8},{1,17},{9,25},{17,1},{25,9},{2,18},{10... | collective-permute-start | bytes 786440 | tf_op jit(solution)/shard_map/ppermute | solution.py:158
  58.9 15.4 %collective-permute-start.15 = (bf16[4,16,2048]{2,1,0:T(8,128)(2,1)S(1)}, bf16[4,16,2048]{2,1,0:T(8,128)(2,1)S(1)}, u32[]{:S(2)}, u32[]{:S(2)}) collective-permute-start(bf16[4,16,2048]{2,1,0:T(8,128)(2,1)S(1)} %get-tuple-element.67), channel_id=1, source_target_pairs={{0,24},{8,16},{16,8},{24,0},{1,25},{9,17},{17,9},{25,1},{2,26},{10... | collective-permute-start | bytes 786440 | tf_op jit(solution)/shard_map/ppermute | solution.py:158
  75.0 3.6 %collective-permute-start.16 = (bf16[4,32,2048]{2,1,0:T(8,128)(2,1)S(1)}, bf16[4,32,2048]{2,1,0:T(8,128)(2,1)S(1)}, u32[]{:S(2)}, u32[]{:S(2)}) collective-permute-start(bf16[4,32,2048]{2,1,0:T(8,128)(2,1)S(1)} %get-tuple-element.69), channel_id=1, source_target_pairs={{0,1},{1,0},{2,3},{3,2},{4,5},{5,4},{6,7},{7,6},{8,9},{9,8},{10,11... | collective-permute-start | bytes 1572872 | tf_op jit(solution)/shard_map/ppermute | solution.py:158
  75.1 9.2 %collective-permute-start.20 = (bf16[4,16,2048]{2,1,0:T(8,128)(2,1)S(1)}, bf16[4,16,2048]{2,1,0:T(8,128)(2,1)S(1)}, u32[]{:S(2)}, u32[]{:S(2)}) collective-permute-start(bf16[4,16,2048]{2,1,0:T(8,128)(2,1)S(1)} %get-tuple-element.61), channel_id=1, source_target_pairs={{0,8},{8,0},{16,24},{24,16},{1,9},{9,1},{17,25},{25,17},{2,10},{10... | collective-permute-start | bytes 786440 | tf_op jit(solution)/shard_map/ppermute | solution.py:158
  76.6 14.0 %collective-permute-start.21 = (bf16[4,16,2048]{2,1,0:T(8,128)(2,1)S(1)}, bf16[4,16,2048]{2,1,0:T(8,128)(2,1)S(1)}, u32[]{:S(2)}, u32[]{:S(2)}) collective-permute-start(bf16[4,16,2048]{2,1,0:T(8,128)(2,1)S(1)} %get-tuple-element.62), channel_id=1, source_target_pairs={{0,16},{8,24},{16,0},{24,8},{1,17},{9,25},{17,1},{25,9},{2,18},{10... | collective-permute-start | bytes 786440 | tf_op jit(solution)/shard_map/ppermute | solution.py:158
  77.2 13.6 %collective-permute-start.22 = (bf16[4,16,2048]{2,1,0:T(8,128)(2,1)S(1)}, bf16[4,16,2048]{2,1,0:T(8,128)(2,1)S(1)}, u32[]{:S(2)}, u32[]{:S(2)}) collective-permute-start(bf16[4,16,2048]{2,1,0:T(8,128)(2,1)S(1)} %get-tuple-element.63), channel_id=1, source_target_pairs={{0,24},{8,16},{16,8},{24,0},{1,25},{9,17},{17,9},{25,1},{2,26},{10... | collective-permute-start | bytes 786440 | tf_op jit(solution)/shard_map/ppermute | solution.py:158
  78.8 12.6 %collective-permute-start.17 = (bf16[32,2048]{1,0:T(8,128)(2,1)S(1)}, bf16[32,2048]{1,0:T(8,128)(2,1)S(1)}, u32[]{:S(2)}, u32[]{:S(2)}) collective-permute-start(bf16[32,2048]{1,0:T(8,128)(2,1)S(1)} %get-tuple-element.84), channel_id=1, source_target_pairs={{0,2},{1,3},{2,0},{3,1},{4,6},{5,7},{6,4},{7,5},{8,10},{9,11},{10,... | collective-permute-start | bytes 393224 | tf_op jit(solution)/shard_map/ppermute | solution.py:158
  78.9 12.5 %collective-permute-start.19 = (bf16[32,2048]{1,0:T(8,128)(2,1)S(1)}, bf16[32,2048]{1,0:T(8,128)(2,1)S(1)}, u32[]{:S(2)}, u32[]{:S(2)}) collective-permute-start(bf16[32,2048]{1,0:T(8,128)(2,1)S(1)} %get-tuple-element.85), channel_id=1, source_target_pairs={{0,6},{1,7},{2,4},{3,5},{4,2},{5,3},{6,0},{7,1},{8,14},{9,15},{10,... | collective-permute-start | bytes 393224 | tf_op jit(solution)/shard_map/ppermute | solution.py:158
  84.3 9.4 %collective-permute-start.18 = (bf16[32,2048]{1,0:T(8,128)(2,1)S(1)}, bf16[32,2048]{1,0:T(8,128)(2,1)S(1)}, u32[]{:S(2)}, u32[]{:S(2)}) collective-permute-start(bf16[32,2048]{1,0:T(8,128)(2,1)S(1)} %get-tuple-element.86), channel_id=1, source_target_pairs={{0,4},{1,5},{2,6},{3,7},{4,0},{5,1},{6,2},{7,3},{8,12},{9,13},{10,... | collective-permute-start | bytes 393224 | tf_op jit(solution)/shard_map/ppermute | solution.py:158
  91.3 3.2 %collective-permute-start.23 = (bf16[4,32,2048]{2,1,0:T(8,128)(2,1)S(1)}, bf16[4,32,2048]{2,1,0:T(8,128)(2,1)S(1)}, u32[]{:S(2)}, u32[]{:S(2)}) collective-permute-start(bf16[4,32,2048]{2,1,0:T(8,128)(2,1)S(1)} %get-tuple-element.75), channel_id=1, source_target_pairs={{0,1},{1,0},{2,3},{3,2},{4,5},{5,4},{6,7},{7,6},{8,9},{9,8},{10,11... | collective-permute-start | bytes 1572872 | tf_op jit(solution)/shard_map/ppermute | solution.py:158
  94.5 13.4 %collective-permute-start.24 = (bf16[32,2048]{1,0:T(8,128)(2,1)S(1)}, bf16[32,2048]{1,0:T(8,128)(2,1)S(1)}, u32[]{:S(2)}, u32[]{:S(2)}) collective-permute-start(bf16[32,2048]{1,0:T(8,128)(2,1)S(1)} %get-tuple-element.81), channel_id=1, source_target_pairs={{0,2},{1,3},{2,0},{3,1},{4,6},{5,7},{6,4},{7,5},{8,10},{9,11},{10,... | collective-permute-start | bytes 393224 | tf_op jit(solution)/shard_map/ppermute | solution.py:158
  96.3 11.7 %collective-permute-start.26 = (bf16[32,2048]{1,0:T(8,128)(2,1)S(1)}, bf16[32,2048]{1,0:T(8,128)(2,1)S(1)}, u32[]{:S(2)}, u32[]{:S(2)}) collective-permute-start(bf16[32,2048]{1,0:T(8,128)(2,1)S(1)} %get-tuple-element.82), channel_id=1, source_target_pairs={{0,6},{1,7},{2,4},{3,5},{4,2},{5,3},{6,0},{7,1},{8,14},{9,15},{10,... | collective-permute-start | bytes 393224 | tf_op jit(solution)/shard_map/ppermute | solution.py:158
  97.6 12.1 %collective-permute-start.25 = (bf16[32,2048]{1,0:T(8,128)(2,1)S(1)}, bf16[32,2048]{1,0:T(8,128)(2,1)S(1)}, u32[]{:S(2)}, u32[]{:S(2)}) collective-permute-start(bf16[32,2048]{1,0:T(8,128)(2,1)S(1)} %get-tuple-element.83), channel_id=1, source_target_pairs={{0,4},{1,5},{2,6},{3,7},{4,0},{5,1},{6,2},{7,3},{8,12},{9,13},{10,... | collective-permute-start | bytes 393224 | tf_op jit(solution)/shard_map/ppermute | solution.py:158

commit v3 on v2

--- a/solution.py
+++ b/solution.py
@@ -439,7 +439,7 @@
         return sums[0], [sums[z].astype(bf16) for z in (1, 2, 3)]
 
     def finish(total, parts):
-        for z in (1, 2, 3):
+        for z in (3, 2, 1):
             total = total + swap(parts[z - 1], "inner", PLACES, 2 * z).astype(f32)
         return total.astype(bf16)
 

time: 111 us -> 110 us (level)
  waiting for transfers between devices: 16.8 us -> 15.4 us
    ppermute x27, waiting for transfers between devices: 16.8 us -> 15.4 us  [swap(): return lax.ppermute(value, axis, [(k, k ^ mask) for k in range(size)])]
  transfers between devices with their start and end apart: 27 -> 27, of which waited for: 10 -> 10; matrix products, arithmetic and copies ran while one was open for 1% -> 1% of each run, Pallas kernels for 46% -> 47%
where the time goes in v3:
time: 110 us
  Pallas kernels  54.7 us (50%)
  starting transfers between devices  27.7 us (25%)
  waiting for transfers between devices  15.4 us (14%)
  local copies, waits for them, and re-layouts  9.56 us (9%)
  other arithmetic  1.75 us (2%)
    ppermute x27, starting transfers between devices, swap(): return lax.ppermute(value, axis, [(k, k ^ mask) for k in range(size)])  27.7 us
    ppermute x27, waiting for transfers between devices, swap(): return lax.ppermute(value, axis, [(k, k ^ mask) for k in range(size)])  15.4 us
    pallas_call x3, Pallas kernels, loaded(): pl.pallas_call(load_kernel, name=name, out_shape=pltpu.VMEM(weight.shape,...  14 us
    pallas_call x1, Pallas kernels, on_device(): pl.pallas_call(backward_kernel, name='backward', out_shape=[hid(bf16), hi...  13.5 us
    pallas_call x1, Pallas kernels, on_device(): pl.pallas_call(up_grads_kernel, name='up_grads', grid=(local,), out_shape...  9.85 us
    unnamed x12, local copies, waits for them, and re-layouts  9.56 us
    pallas_call x1, Pallas kernels, on_device(): pl.pallas_call(forward_kernel, name='forward', out_shape=[hid(f32), hid(f...  7.14 us
    pallas_call x1, Pallas kernels, on_device(): pl.pallas_call(down_grads_kernel, name='down_grads', grid=(local,), out_s...  6.37 us
  transfers between devices with their start and end apart: 27, of which 10 were waited for; matrix products, arithmetic and copies ran while one was open for 1% of the time, Pallas kernels for 47%

profile of v3, /device:TPU:0, one launch (start us, length us, event | category | flops | bytes accessed | tf_op | source)
XLA Modules:
  0.0 109.9 jit_solution(9467174416291054552)
XLA Ops:
  0.6 1.1 pack.1.refs_0_
  1.7 5.1 %collective-permute-start.4 = (bf16[32,4224]{1,0:T(8,128)(2,1)S(1)}, bf16[32,4224]{1,0:T(8,128)(2,1)S(1)}, u32[]{:S(2)}, u32[]{:S(2)}) collective-permute-start(bf16[32,4224]{1,0:T(8,128)(2,1)S(1)} %pack.1.refs_0_), channel_id=1, source_target_pairs={{0,6},{1,7},{2,4},{3,5},{4,2},{5,3},{6,0},{7,1},{8,14},{9,15},{10,... | collective-permute-start | bytes 811016 | tf_op jit(solution)/shard_map/ppermute | solution.py:158
  6.8 0.6 collective-permute-start.1
  7.4 4.6 %load_gate.1.refs_4_.refs_6_ = bf16[1,4,2048,768]{3,2,1,0:T(8,128)(2,1)S(1)} custom-call(bf16[1,4,2048,768]{3,2,1,0:T(8,128)(2,1)} %source_ref.3), custom_call_target="tpu_custom_call" | custom-call | bytes 25165824 | tf_op jit(solution)/shard_map/load_gate/pallas_call | solution.py:344
  12.0 0.0 copy-start
  12.0 4.8 %copy-done = bf16[1,4,2048,768]{3,2,1,0:T(8,128)(2,1)} copy-done((bf16[1,4,2048,768]{3,2,1,0:T(8,128)(2,1)}, bf16[1,4,2048,768]{3,2,1,0:T(8,128)(2,1)S(1)}, u32[]{:S(2)}) %copy-start) | copy-done | bytes 12582936
  16.8 4.6 %load_up.1.refs_5_.refs_7_ = bf16[1,4,2048,768]{3,2,1,0:T(8,128)(2,1)S(1)} custom-call(bf16[1,4,2048,768]{3,2,1,0:T(8,128)(2,1)} %source_ref.4), custom_call_target="tpu_custom_call" | custom-call | bytes 25165824 | tf_op jit(solution)/shard_map/load_up/pallas_call | solution.py:344
  21.4 0.0 copy-start.1
  21.4 4.8 %copy-done.1 = bf16[1,4,2048,768]{3,2,1,0:T(8,128)(2,1)} copy-done((bf16[1,4,2048,768]{3,2,1,0:T(8,128)(2,1)}, bf16[1,4,2048,768]{3,2,1,0:T(8,128)(2,1)S(1)}, u32[]{:S(2)}) %copy-start.1) | copy-done | bytes 12582936
  26.2 0.0 collective-permute-done.4.refs_6_
  26.2 3.6 %collective-permute-done.3.refs_4_ = bf16[32,4224]{1,0:T(8,128)(2,1)S(1)} collective-permute-done((bf16[32,4224]{1,0:T(8,128)(2,1)S(1)}, bf16[32,4224]{1,0:T(8,128)(2,1)S(1)}, u32[]{:S(2)}, u32[]{:S(2)}) %collective-permute-start.3) | collective-permute-done | bytes 270368 | tf_op jit(solution)/shard_map/ppermute | solution.py:158
  29.8 0.5 collective-permute-start.2
  30.3 0.0 collective-permute-start.6
  30.3 0.1 pad_add_fusion.place_ref
  30.4 0.0 collective-permute-done.refs_1_
  30.4 1.3 %collective-permute-done.2.refs_3_ = bf16[32,4224]{1,0:T(8,128)(2,1)S(1)} collective-permute-done((bf16[32,4224]{1,0:T(8,128)(2,1)S(1)}, bf16[32,4224]{1,0:T(8,128)(2,1)S(1)}, u32[]{:S(2)}, u32[]{:S(2)}) %collective-permute-start.2) | collective-permute-done | bytes 270368 | tf_op jit(solution)/shard_map/ppermute | solution.py:158
  31.7 0.4 collective-permute-done.6.refs_7_
  32.1 1.6 %select.1 = (bf16[4,16,2048]{2,1,0:T(8,128)(2,1)S(1)}, bf16[4,16,2048]{2,1,0:T(8,128)(2,1)S(1)}, bf16[4,16,2048]{2,1,0:T(8,128)(2,1)S(1)}, bf16[4,16,2048]{2,1,0...) custom-call(s32[2]{0:T(128)S(1)} %pad_add_fusion.place_ref, ...), custom_call_target="tpu_custom_call" | custom-call | flops 536870912 | bytes 4194304 | tf_op jit(solution)/shard_map/select/pallas_call | solution.py:386
  33.7 1.6 %collective-permute-start.7 = (bf16[4,16,2048]{2,1,0:T(8,128)(2,1)S(1)}, bf16[4,16,2048]{2,1,0:T(8,128)(2,1)S(1)}, u32[]{:S(2)}, u32[]{:S(2)}) collective-permute-start(bf16[4,16,2048]{2,1,0:T(8,128)(2,1)S(1)} %get-tuple-element.48), channel_id=1, source_target_pairs={{0,8},{8,0},{16,24},{24,16},{1,9},{9,1},{17,25},{25,17},{2,10},{10... | collective-permute-start | bytes 786440 | tf_op jit(solution)/shard_map/ppermute | solution.py:158
  35.3 1.5 %collective-permute-start.8 = (bf16[4,16,2048]{2,1,0:T(8,128)(2,1)S(1)}, bf16[4,16,2048]{2,1,0:T(8,128)(2,1)S(1)}, u32[]{:S(2)}, u32[]{:S(2)}) collective-permute-start(bf16[4,16,2048]{2,1,0:T(8,128)(2,1)S(1)} %get-tuple-element.49), channel_id=1, source_target_pairs={{0,16},{8,24},{16,0},{24,8},{1,17},{9,25},{17,1},{25,9},{2,18},{10... | collective-permute-start | bytes 786440 | tf_op jit(solution)/shard_map/ppermute | solution.py:158
  36.8 0.5 collective-permute-start.9
  37.3 4.9 %load_down.1.refs_6_.refs_8_ = bf16[1,4,768,2048]{3,2,1,0:T(8,128)(2,1)S(1)} custom-call(bf16[1,4,768,2048]{3,2,1,0:T(8,128)(2,1)} %source_ref.5), custom_call_target="tpu_custom_call" | custom-call | bytes 25165824 | tf_op jit(solution)/shard_map/load_down/pallas_call | solution.py:344
  42.2 2.0 %collective-permute-start.10 = (bf16[4,16,2048]{2,1,0:T(8,128)(2,1)S(1)}, bf16[4,16,2048]{2,1,0:T(8,128)(2,1)S(1)}, u32[]{:S(2)}, u32[]{:S(2)}) collective-permute-start(bf16[4,16,2048]{2,1,0:T(8,128)(2,1)S(1)} %get-tuple-element.55), channel_id=1, source_target_pairs={{0,8},{8,0},{16,24},{24,16},{1,9},{9,1},{17,25},{25,17},{2,10},{10... | collective-permute-start | bytes 786440 | tf_op jit(solution)/shard_map/ppermute | solution.py:158
  44.2 1.6 %collective-permute-start.11 = (bf16[4,16,2048]{2,1,0:T(8,128)(2,1)S(1)}, bf16[4,16,2048]{2,1,0:T(8,128)(2,1)S(1)}, u32[]{:S(2)}, u32[]{:S(2)}) collective-permute-start(bf16[4,16,2048]{2,1,0:T(8,128)(2,1)S(1)} %get-tuple-element.56), channel_id=1, source_target_pairs={{0,16},{8,24},{16,0},{24,8},{1,17},{9,25},{17,1},{25,9},{2,18},{10... | collective-permute-start | bytes 786440 | tf_op jit(solution)/shard_map/ppermute | solution.py:158
  45.8 0.0 collective-permute-done.7.refs_1_
  45.8 0.0 collective-permute-start.12
  45.8 3.3 %collective-permute-done.8.refs_2_ = bf16[4,16,2048]{2,1,0:T(8,128)(2,1)S(1)} collective-permute-done((bf16[4,16,2048]{2,1,0:T(8,128)(2,1)S(1)}, bf16[4,16,2048]{2,1,0:T(8,128)(2,1)S(1)}, u32[]{:S(2)}, u32[]{:S(2)}) %collective-permute-start.8) | collective-permute-done | bytes 262176 | tf_op jit(solution)/shard_map/ppermute | solution.py:158
  49.1 0.4 collective-permute-done.9.refs_3_
  49.6 7.1 %forward.1 = (f32[4,64,768]{2,1,0:T(8,128)S(1)}, f32[4,64,768]{2,1,0:T(8,128)S(1)}, bf16[4,64,768]{2,1,0:T(8,128)(2,1)S(1)}, bf16[4,16,2048]{2,1,0:T(8,128)(2,1)...) custom-call(bf16[4,16,2048]{2,1,0:T(8,128)(2,1)S(1)} %get-tuple-element.4, ...), custom_call_target="tpu_custom_call" | custom-call | flops 9663676416 | bytes 37748736 | tf_op jit(solution)/shard_map/forward/pallas_call | solution.py:403
  56.7 1.6 %collective-permute-start.13 = (bf16[4,16,2048]{2,1,0:T(8,128)(2,1)S(1)}, bf16[4,16,2048]{2,1,0:T(8,128)(2,1)S(1)}, u32[]{:S(2)}, u32[]{:S(2)}) collective-permute-start(bf16[4,16,2048]{2,1,0:T(8,128)(2,1)S(1)} %get-tuple-element.65), channel_id=1, source_target_pairs={{0,8},{8,0},{16,24},{24,16},{1,9},{9,1},{17,25},{25,17},{2,10},{10... | collective-permute-start | bytes 786440 | tf_op jit(solution)/shard_map/ppermute | solution.py:158
  58.3 0.6 collective-permute-start.14
  58.9 1.4 %collective-permute-start.15 = (bf16[4,16,2048]{2,1,0:T(8,128)(2,1)S(1)}, bf16[4,16,2048]{2,1,0:T(8,128)(2,1)S(1)}, u32[]{:S(2)}, u32[]{:S(2)}) collective-permute-start(bf16[4,16,2048]{2,1,0:T(8,128)(2,1)S(1)} %get-tuple-element.67), channel_id=1, source_target_pairs={{0,24},{8,16},{16,8},{24,0},{1,25},{9,17},{17,9},{25,1},{2,26},{10... | collective-permute-start | bytes 786440 | tf_op jit(solution)/shard_map/ppermute | solution.py:158
  60.3 0.0 collective-permute-done.11.refs_2_
  60.3 0.5 collective-permute-done.12.refs_3_
  60.8 13.5 %backward.1 = (bf16[4,64,768]{2,1,0:T(8,128)(2,1)S(1)}, bf16[4,64,768]{2,1,0:T(8,128)(2,1)S(1)}, bf16[4,16,2048]{2,1,0:T(8,128)(2,1)S(1)}, bf16[4,16,2048]{2,1,0...) custom-call(bf16[4,16,2048]{2,1,0:T(8,128)(2,1)S(1)} %get-tuple-element.54.refs_0_, ...), custom_call_target="tpu_custom_call" | custom-call | flops 9663676416 | bytes 37748736 | tf_op jit(solution)/shard_map/backward/pallas_call | solution.py:414
  74.3 0.0 collective-permute-done.13.refs_3_
  74.3 0.0 collective-permute-done.14.refs_4_
  74.3 0.7 combine_out.1
  75.0 0.1 collective-permute-start.16
  75.1 1.5 %collective-permute-start.20 = (bf16[4,16,2048]{2,1,0:T(8,128)(2,1)S(1)}, bf16[4,16,2048]{2,1,0:T(8,128)(2,1)S(1)}, u32[]{:S(2)}, u32[]{:S(2)}) collective-permute-start(bf16[4,16,2048]{2,1,0:T(8,128)(2,1)S(1)} %get-tuple-element.61), channel_id=1, source_target_pairs={{0,8},{8,0},{16,24},{24,16},{1,9},{9,1},{17,25},{25,17},{2,10},{10... | collective-permute-start | bytes 786440 | tf_op jit(solution)/shard_map/ppermute | solution.py:158
  76.6 0.6 collective-permute-start.21
  77.2 1.5 %collective-permute-start.22 = (bf16[4,16,2048]{2,1,0:T(8,128)(2,1)S(1)}, bf16[4,16,2048]{2,1,0:T(8,128)(2,1)S(1)}, u32[]{:S(2)}, u32[]{:S(2)}) collective-permute-start(bf16[4,16,2048]{2,1,0:T(8,128)(2,1)S(1)} %get-tuple-element.63), channel_id=1, source_target_pairs={{0,24},{8,16},{16,8},{24,0},{1,25},{9,17},{17,9},{25,1},{2,26},{10... | collective-permute-start | bytes 786440 | tf_op jit(solution)/shard_map/ppermute | solution.py:158
  78.7 0.0 collective-permute-done.16
  78.7 0.1 fusion.6
  78.8 2.5 %collective-permute-start.17 = (bf16[32,2048]{1,0:T(8,128)(2,1)S(1)}, bf16[32,2048]{1,0:T(8,128)(2,1)S(1)}, u32[]{:S(2)}, u32[]{:S(2)}) collective-permute-start(bf16[32,2048]{1,0:T(8,128)(2,1)S(1)} %get-tuple-element.84), channel_id=1, source_target_pairs={{0,6},{1,7},{2,4},{3,5},{4,2},{5,3},{6,0},{7,1},{8,14},{9,15},{10,... | collective-permute-start | bytes 393224 | tf_op jit(solution)/shard_map/ppermute | solution.py:158
  81.3 0.0 collective-permute-start.19
  81.3 3.0 %collective-permute-done.20.refs_2_ = bf16[4,16,2048]{2,1,0:T(8,128)(2,1)S(1)} collective-permute-done((bf16[4,16,2048]{2,1,0:T(8,128)(2,1)S(1)}, bf16[4,16,2048]{2,1,0:T(8,128)(2,1)S(1)}, u32[]{:S(2)}, u32[]{:S(2)}) %collective-permute-start.20) | collective-permute-done | bytes 262176 | tf_op jit(solution)/shard_map/ppermute | solution.py:158
  84.3 6.4 %down_grads.1 = bf16[1,4,768,2048]{3,2,1,0:T(8,128)(2,1)} custom-call(bf16[4,16,2048]{2,1,0:T(8,128)(2,1)S(1)} %get-tuple-element.54.refs_0_, bf16[4,16,2048]{2,1,0:T(8,128)(2,1)S(1)} %collective-permute-done.10.refs_1_, bf16[4,16,2048]{2,1,0:T(8,128)(2,1)S(1)} %collective-permute-done.11.refs_2_, bf16[4,16,2048]{2,1,0:T(8,128)(2,1)S(1)} %collective-permute-done.12.refs_3_, ...), custom_call_target="tpu_custom_call" | custom-call | flops 3221225472 | bytes 12582912 | tf_op jit(solution)/shard_map/down_grads/pallas_call | solution.py:453
  90.7 0.0 collective-permute-done.21.refs_3_
  90.7 0.2 collective-permute-done.22.refs_4_
  90.8 0.4 combine_dx.1
  91.3 0.1 collective-permute-start.23
  91.4 0.0 collective-permute-done.17
  91.4 0.0 collective-permute-done.19
  91.4 1.2 %collective-permute-done.18 = bf16[32,2048]{1,0:T(8,128)(2,1)S(1)} collective-permute-done((bf16[32,2048]{1,0:T(8,128)(2,1)S(1)}, bf16[32,2048]{1,0:T(8,128)(2,1)S(1)}, u32[]{:S(2)}, u32[]{:S(2)}) %collective-permute-start.18) | collective-permute-done | bytes 131104 | tf_op jit(solution)/shard_map/ppermute | solution.py:158
  92.6 0.7 fusion.5
  93.4 0.0 collective-permute-done.23
  93.4 0.1 fusion.9
  93.5 2.5 %collective-permute-start.24 = (bf16[32,2048]{1,0:T(8,128)(2,1)S(1)}, bf16[32,2048]{1,0:T(8,128)(2,1)S(1)}, u32[]{:S(2)}, u32[]{:S(2)}) collective-permute-start(bf16[32,2048]{1,0:T(8,128)(2,1)S(1)} %get-tuple-element.81), channel_id=1, source_target_pairs={{0,6},{1,7},{2,4},{3,5},{4,2},{5,3},{6,0},{7,1},{8,14},{9,15},{10,... | collective-permute-start | bytes 393224 | tf_op jit(solution)/shard_map/ppermute | solution.py:158
  96.0 0.7 collective-permute-start.26
  96.7 1.2 %collective-permute-start.25 = (bf16[32,2048]{1,0:T(8,128)(2,1)S(1)}, bf16[32,2048]{1,0:T(8,128)(2,1)S(1)}, u32[]{:S(2)}, u32[]{:S(2)}) collective-permute-start(bf16[32,2048]{1,0:T(8,128)(2,1)S(1)} %get-tuple-element.83), channel_id=1, source_target_pairs={{0,4},{1,5},{2,6},{3,7},{4,0},{5,1},{6,2},{7,3},{8,12},{9,13},{10,... | collective-permute-start | bytes 393224 | tf_op jit(solution)/shard_map/ppermute | solution.py:158
  97.9 9.9 %up_grads.1 = (bf16[1,4,2048,768]{3,2,1,0:T(8,128)(2,1)}, bf16[1,4,2048,768]{3,2,1,0:T(8,128)(2,1)}) custom-call(bf16[4,16,2048]{2,1,0:T(8,128)(2,1)S(1)} %get-tuple-element.47.refs_0_, bf16[4,16,2048]{2,1,0:T(8,128)(2,1)S(1)} %collective-permute-done.7.refs_1_, bf16[4,16,2048]{2,1,0:T(8,128)(2,1)S(1)} %collective-permute-done.8.refs_2_, ...), custom_call_target="tpu_custom_call" | custom-call | flops 6442450944 | bytes 25165824 | tf_op jit(solution)/shard_map/up_grads/pallas_call | solution.py:466
  107.8 1.4 %collective-permute-done.25 = bf16[32,2048]{1,0:T(8,128)(2,1)S(1)} collective-permute-done((bf16[32,2048]{1,0:T(8,128)(2,1)S(1)}, bf16[32,2048]{1,0:T(8,128)(2,1)S(1)}, u32[]{:S(2)}, u32[]{:S(2)}) %collective-permute-start.25) | collective-permute-done | bytes 131104 | tf_op jit(solution)/shard_map/ppermute | solution.py:158
  109.2 0.7 fusion.2
  (19 shorter events, 0.0 us)
Async XLA Ops:
  1.7 24.5 %collective-permute-start.4 = (bf16[32,4224]{1,0:T(8,128)(2,1)S(1)}, bf16[32,4224]{1,0:T(8,128)(2,1)S(1)}, u32[]{:S(2)}, u32[]{:S(2)}) collective-permute-start(bf16[32,4224]{1,0:T(8,128)(2,1)S(1)} %pack.1.refs_0_), channel_id=1, source_target_pairs={{0,6},{1,7},{2,4},{3,5},{4,2},{5,3},{6,0},{7,1},{8,14},{9,15},{10,... | collective-permute-start | bytes 811016 | tf_op jit(solution)/shard_map/ppermute | solution.py:158
  6.8 23.0 %collective-permute-start.3 = (bf16[32,4224]{1,0:T(8,128)(2,1)S(1)}, bf16[32,4224]{1,0:T(8,128)(2,1)S(1)}, u32[]{:S(2)}, u32[]{:S(2)}) collective-permute-start(bf16[32,4224]{1,0:T(8,128)(2,1)S(1)} %pack.1.refs_0_), channel_id=1, source_target_pairs={{0,4},{1,5},{2,6},{3,7},{4,0},{5,1},{6,2},{7,3},{8,12},{9,13},{10,... | collective-permute-start | bytes 811016 | tf_op jit(solution)/shard_map/ppermute | solution.py:158
  6.8 23.0 %collective-permute-start.1 = (bf16[32,4224]{1,0:T(8,128)(2,1)S(1)}, bf16[32,4224]{1,0:T(8,128)(2,1)S(1)}, u32[]{:S(2)}, u32[]{:S(2)}) collective-permute-start(bf16[32,4224]{1,0:T(8,128)(2,1)S(1)} %pack.1.refs_0_), channel_id=1, source_target_pairs={{0,2},{1,3},{2,0},{3,1},{4,6},{5,7},{6,4},{7,5},{8,10},{9,11},{10,... | collective-permute-start | bytes 811016 | tf_op jit(solution)/shard_map/ppermute | solution.py:158
  7.4 23.0 %collective-permute-start = (bf16[32,4224]{1,0:T(8,128)(2,1)S(1)}, bf16[32,4224]{1,0:T(8,128)(2,1)S(1)}, u32[]{:S(2)}, u32[]{:S(2)}) collective-permute-start(bf16[32,4224]{1,0:T(8,128)(2,1)S(1)} %pack.1.refs_0_), channel_id=1, source_target_pairs={{0,1},{1,0},{2,3},{3,2},{4,5},{5,4},{6,7},{7,6},{8,9},{9,8},{10,11... | collective-permute-start | bytes 811016 | tf_op jit(solution)/shard_map/ppermute | solution.py:158
  12.0 4.8 %copy-start = (bf16[1,4,2048,768]{3,2,1,0:T(8,128)(2,1)}, bf16[1,4,2048,768]{3,2,1,0:T(8,128)(2,1)S(1)}, u32[]{:S(2)}) copy-start(bf16[1,4,2048,768]{3,2,1,0:T(8,128)(2,1)S(1)} %load_gate.1.refs_4_.refs_6_) | copy-start | bytes 37748740
  21.4 4.8 %copy-start.1 = (bf16[1,4,2048,768]{3,2,1,0:T(8,128)(2,1)}, bf16[1,4,2048,768]{3,2,1,0:T(8,128)(2,1)S(1)}, u32[]{:S(2)}) copy-start(bf16[1,4,2048,768]{3,2,1,0:T(8,128)(2,1)S(1)} %load_up.1.refs_5_.refs_7_) | copy-start | bytes 37748740
  29.8 1.9 %collective-permute-start.5 = (bf16[32,4224]{1,0:T(8,128)(2,1)S(1)}, bf16[32,4224]{1,0:T(8,128)(2,1)S(1)}, u32[]{:S(2)}, u32[]{:S(2)}) collective-permute-start(bf16[32,4224]{1,0:T(8,128)(2,1)S(1)} %collective-permute-done.3.refs_4_), channel_id=1, source_target_pairs={{0,1},{1,0},{2,3},{3,2},{4,5},{5,4},{6,7},{7,6},{8,9},{9,8},{10,11... | collective-permute-start | bytes 811016 | tf_op jit(solution)/shard_map/ppermute | solution.py:158
  29.8 1.9 %collective-permute-start.2 = (bf16[32,4224]{1,0:T(8,128)(2,1)S(1)}, bf16[32,4224]{1,0:T(8,128)(2,1)S(1)}, u32[]{:S(2)}, u32[]{:S(2)}) collective-permute-start(bf16[32,4224]{1,0:T(8,128)(2,1)S(1)} %collective-permute-done.1.refs_2_), channel_id=1, source_target_pairs={{0,1},{1,0},{2,3},{3,2},{4,5},{5,4},{6,7},{7,6},{8,9},{9,8},{10,11... | collective-permute-start | bytes 811016 | tf_op jit(solution)/shard_map/ppermute | solution.py:158
  30.3 1.8 %collective-permute-start.6 = (bf16[32,4224]{1,0:T(8,128)(2,1)S(1)}, bf16[32,4224]{1,0:T(8,128)(2,1)S(1)}, u32[]{:S(2)}, u32[]{:S(2)}) collective-permute-start(bf16[32,4224]{1,0:T(8,128)(2,1)S(1)} %collective-permute-done.4.refs_6_), channel_id=1, source_target_pairs={{0,1},{1,0},{2,3},{3,2},{4,5},{5,4},{6,7},{7,6},{8,9},{9,8},{10,11... | collective-permute-start | bytes 811016 | tf_op jit(solution)/shard_map/ppermute | solution.py:158
  33.7 12.1 %collective-permute-start.7 = (bf16[4,16,2048]{2,1,0:T(8,128)(2,1)S(1)}, bf16[4,16,2048]{2,1,0:T(8,128)(2,1)S(1)}, u32[]{:S(2)}, u32[]{:S(2)}) collective-permute-start(bf16[4,16,2048]{2,1,0:T(8,128)(2,1)S(1)} %get-tuple-element.48), channel_id=1, source_target_pairs={{0,8},{8,0},{16,24},{24,16},{1,9},{9,1},{17,25},{25,17},{2,10},{10... | collective-permute-start | bytes 786440 | tf_op jit(solution)/shard_map/ppermute | solution.py:158
  35.3 13.8 %collective-permute-start.8 = (bf16[4,16,2048]{2,1,0:T(8,128)(2,1)S(1)}, bf16[4,16,2048]{2,1,0:T(8,128)(2,1)S(1)}, u32[]{:S(2)}, u32[]{:S(2)}) collective-permute-start(bf16[4,16,2048]{2,1,0:T(8,128)(2,1)S(1)} %get-tuple-element.49), channel_id=1, source_target_pairs={{0,16},{8,24},{16,0},{24,8},{1,17},{9,25},{17,1},{25,9},{2,18},{10... | collective-permute-start | bytes 786440 | tf_op jit(solution)/shard_map/ppermute | solution.py:158
  36.8 12.8 %slice-start = ((s8[12582912]{0:T(1024)(128)(4,1)}), s8[4194304]{0:T(1024)(128)(4,1)S(1)}, s32[]{:S(2)}) async-start(s8[12582912]{0:T(1024)(128)(4,1)} %bitcast.33), calls=%async_computation | async-start | bytes 8388608
  36.8 12.8 %slice-start.1 = ((s8[12582912]{0:T(1024)(128)(4,1)}), s8[4194304]{0:T(1024)(128)(4,1)S(1)}, s32[]{:S(2)}) async-start(s8[12582912]{0:T(1024)(128)(4,1)} %bitcast.33), calls=%async_computation.1 | async-start | bytes 8388608
  36.8 12.8 %slice-start.2 = ((s8[12582912]{0:T(1024)(128)(4,1)}), s8[4194304]{0:T(1024)(128)(4,1)S(1)}, s32[]{:S(2)}) async-start(s8[12582912]{0:T(1024)(128)(4,1)} %bitcast.33), calls=%async_computation.2 | async-start | bytes 8388608
  36.8 12.8 %copy-start.2 = (bf16[1,4,2048,768]{3,2,1,0:T(8,128)(2,1)S(1)}, bf16[1,4,2048,768]{3,2,1,0:T(8,128)(2,1)}, u32[]{:S(2)}) copy-start(bf16[1,4,2048,768]{3,2,1,0:T(8,128)(2,1)} %copy-done.1) | copy-start | bytes 37748740
  36.8 12.7 %collective-permute-start.9 = (bf16[4,16,2048]{2,1,0:T(8,128)(2,1)S(1)}, bf16[4,16,2048]{2,1,0:T(8,128)(2,1)S(1)}, u32[]{:S(2)}, u32[]{:S(2)}) collective-permute-start(bf16[4,16,2048]{2,1,0:T(8,128)(2,1)S(1)} %get-tuple-element.50), channel_id=1, source_target_pairs={{0,24},{8,16},{16,8},{24,0},{1,25},{9,17},{17,9},{25,1},{2,26},{10... | collective-permute-start | bytes 786440 | tf_op jit(solution)/shard_map/ppermute | solution.py:158
  42.2 16.7 %collective-permute-start.10 = (bf16[4,16,2048]{2,1,0:T(8,128)(2,1)S(1)}, bf16[4,16,2048]{2,1,0:T(8,128)(2,1)S(1)}, u32[]{:S(2)}, u32[]{:S(2)}) collective-permute-start(bf16[4,16,2048]{2,1,0:T(8,128)(2,1)S(1)} %get-tuple-element.55), channel_id=1, source_target_pairs={{0,8},{8,0},{16,24},{24,16},{1,9},{9,1},{17,25},{25,17},{2,10},{10... | collective-permute-start | bytes 786440 | tf_op jit(solution)/shard_map/ppermute | solution.py:158
  44.2 16.1 %collective-permute-start.11 = (bf16[4,16,2048]{2,1,0:T(8,128)(2,1)S(1)}, bf16[4,16,2048]{2,1,0:T(8,128)(2,1)S(1)}, u32[]{:S(2)}, u32[]{:S(2)}) collective-permute-start(bf16[4,16,2048]{2,1,0:T(8,128)(2,1)S(1)} %get-tuple-element.56), channel_id=1, source_target_pairs={{0,16},{8,24},{16,0},{24,8},{1,17},{9,25},{17,1},{25,9},{2,18},{10... | collective-permute-start | bytes 786440 | tf_op jit(solution)/shard_map/ppermute | solution.py:158
  45.8 15.0 %collective-permute-start.12 = (bf16[4,16,2048]{2,1,0:T(8,128)(2,1)S(1)}, bf16[4,16,2048]{2,1,0:T(8,128)(2,1)S(1)}, u32[]{:S(2)}, u32[]{:S(2)}) collective-permute-start(bf16[4,16,2048]{2,1,0:T(8,128)(2,1)S(1)} %get-tuple-element.57), channel_id=1, source_target_pairs={{0,24},{8,16},{16,8},{24,0},{1,25},{9,17},{17,9},{25,1},{2,26},{10... | collective-permute-start | bytes 786440 | tf_op jit(solution)/shard_map/ppermute | solution.py:158
  56.7 17.6 %collective-permute-start.13 = (bf16[4,16,2048]{2,1,0:T(8,128)(2,1)S(1)}, bf16[4,16,2048]{2,1,0:T(8,128)(2,1)S(1)}, u32[]{:S(2)}, u32[]{:S(2)}) collective-permute-start(bf16[4,16,2048]{2,1,0:T(8,128)(2,1)S(1)} %get-tuple-element.65), channel_id=1, source_target_pairs={{0,8},{8,0},{16,24},{24,16},{1,9},{9,1},{17,25},{25,17},{2,10},{10... | collective-permute-start | bytes 786440 | tf_op jit(solution)/shard_map/ppermute | solution.py:158
  58.3 16.0 %collective-permute-start.14 = (bf16[4,16,2048]{2,1,0:T(8,128)(2,1)S(1)}, bf16[4,16,2048]{2,1,0:T(8,128)(2,1)S(1)}, u32[]{:S(2)}, u32[]{:S(2)}) collective-permute-start(bf16[4,16,2048]{2,1,0:T(8,128)(2,1)S(1)} %get-tuple-element.66), channel_id=1, source_target_pairs={{0,16},{8,24},{16,0},{24,8},{1,17},{9,25},{17,1},{25,9},{2,18},{10... | collective-permute-start | bytes 786440 | tf_op jit(solution)/shard_map/ppermute | solution.py:158
  58.9 15.4 %collective-permute-start.15 = (bf16[4,16,2048]{2,1,0:T(8,128)(2,1)S(1)}, bf16[4,16,2048]{2,1,0:T(8,128)(2,1)S(1)}, u32[]{:S(2)}, u32[]{:S(2)}) collective-permute-start(bf16[4,16,2048]{2,1,0:T(8,128)(2,1)S(1)} %get-tuple-element.67), channel_id=1, source_target_pairs={{0,24},{8,16},{16,8},{24,0},{1,25},{9,17},{17,9},{25,1},{2,26},{10... | collective-permute-start | bytes 786440 | tf_op jit(solution)/shard_map/ppermute | solution.py:158
  75.0 3.6 %collective-permute-start.16 = (bf16[4,32,2048]{2,1,0:T(8,128)(2,1)S(1)}, bf16[4,32,2048]{2,1,0:T(8,128)(2,1)S(1)}, u32[]{:S(2)}, u32[]{:S(2)}) collective-permute-start(bf16[4,32,2048]{2,1,0:T(8,128)(2,1)S(1)} %get-tuple-element.69), channel_id=1, source_target_pairs={{0,1},{1,0},{2,3},{3,2},{4,5},{5,4},{6,7},{7,6},{8,9},{9,8},{10,11... | collective-permute-start | bytes 1572872 | tf_op jit(solution)/shard_map/ppermute | solution.py:158
  75.1 9.2 %collective-permute-start.20 = (bf16[4,16,2048]{2,1,0:T(8,128)(2,1)S(1)}, bf16[4,16,2048]{2,1,0:T(8,128)(2,1)S(1)}, u32[]{:S(2)}, u32[]{:S(2)}) collective-permute-start(bf16[4,16,2048]{2,1,0:T(8,128)(2,1)S(1)} %get-tuple-element.61), channel_id=1, source_target_pairs={{0,8},{8,0},{16,24},{24,16},{1,9},{9,1},{17,25},{25,17},{2,10},{10... | collective-permute-start | bytes 786440 | tf_op jit(solution)/shard_map/ppermute | solution.py:158
  76.6 14.0 %collective-permute-start.21 = (bf16[4,16,2048]{2,1,0:T(8,128)(2,1)S(1)}, bf16[4,16,2048]{2,1,0:T(8,128)(2,1)S(1)}, u32[]{:S(2)}, u32[]{:S(2)}) collective-permute-start(bf16[4,16,2048]{2,1,0:T(8,128)(2,1)S(1)} %get-tuple-element.62), channel_id=1, source_target_pairs={{0,16},{8,24},{16,0},{24,8},{1,17},{9,25},{17,1},{25,9},{2,18},{10... | collective-permute-start | bytes 786440 | tf_op jit(solution)/shard_map/ppermute | solution.py:158
  77.2 13.6 %collective-permute-start.22 = (bf16[4,16,2048]{2,1,0:T(8,128)(2,1)S(1)}, bf16[4,16,2048]{2,1,0:T(8,128)(2,1)S(1)}, u32[]{:S(2)}, u32[]{:S(2)}) collective-permute-start(bf16[4,16,2048]{2,1,0:T(8,128)(2,1)S(1)} %get-tuple-element.63), channel_id=1, source_target_pairs={{0,24},{8,16},{16,8},{24,0},{1,25},{9,17},{17,9},{25,1},{2,26},{10... | collective-permute-start | bytes 786440 | tf_op jit(solution)/shard_map/ppermute | solution.py:158
  78.8 12.6 %collective-permute-start.17 = (bf16[32,2048]{1,0:T(8,128)(2,1)S(1)}, bf16[32,2048]{1,0:T(8,128)(2,1)S(1)}, u32[]{:S(2)}, u32[]{:S(2)}) collective-permute-start(bf16[32,2048]{1,0:T(8,128)(2,1)S(1)} %get-tuple-element.84), channel_id=1, source_target_pairs={{0,6},{1,7},{2,4},{3,5},{4,2},{5,3},{6,0},{7,1},{8,14},{9,15},{10,... | collective-permute-start | bytes 393224 | tf_op jit(solution)/shard_map/ppermute | solution.py:158
  81.3 10.1 %collective-permute-start.19 = (bf16[32,2048]{1,0:T(8,128)(2,1)S(1)}, bf16[32,2048]{1,0:T(8,128)(2,1)S(1)}, u32[]{:S(2)}, u32[]{:S(2)}) collective-permute-start(bf16[32,2048]{1,0:T(8,128)(2,1)S(1)} %get-tuple-element.85), channel_id=1, source_target_pairs={{0,2},{1,3},{2,0},{3,1},{4,6},{5,7},{6,4},{7,5},{8,10},{9,11},{10,... | collective-permute-start | bytes 393224 | tf_op jit(solution)/shard_map/ppermute | solution.py:158
  84.3 8.3 %collective-permute-start.18 = (bf16[32,2048]{1,0:T(8,128)(2,1)S(1)}, bf16[32,2048]{1,0:T(8,128)(2,1)S(1)}, u32[]{:S(2)}, u32[]{:S(2)}) collective-permute-start(bf16[32,2048]{1,0:T(8,128)(2,1)S(1)} %get-tuple-element.86), channel_id=1, source_target_pairs={{0,4},{1,5},{2,6},{3,7},{4,0},{5,1},{6,2},{7,3},{8,12},{9,13},{10,... | collective-permute-start | bytes 393224 | tf_op jit(solution)/shard_map/ppermute | solution.py:158
  91.3 2.1 %collective-permute-start.23 = (bf16[4,32,2048]{2,1,0:T(8,128)(2,1)S(1)}, bf16[4,32,2048]{2,1,0:T(8,128)(2,1)S(1)}, u32[]{:S(2)}, u32[]{:S(2)}) collective-permute-start(bf16[4,32,2048]{2,1,0:T(8,128)(2,1)S(1)} %get-tuple-element.75), channel_id=1, source_target_pairs={{0,1},{1,0},{2,3},{3,2},{4,5},{5,4},{6,7},{7,6},{8,9},{9,8},{10,11... | collective-permute-start | bytes 1572872 | tf_op jit(solution)/shard_map/ppermute | solution.py:158
  93.5 14.3 %collective-permute-start.24 = (bf16[32,2048]{1,0:T(8,128)(2,1)S(1)}, bf16[32,2048]{1,0:T(8,128)(2,1)S(1)}, u32[]{:S(2)}, u32[]{:S(2)}) collective-permute-start(bf16[32,2048]{1,0:T(8,128)(2,1)S(1)} %get-tuple-element.81), channel_id=1, source_target_pairs={{0,6},{1,7},{2,4},{3,5},{4,2},{5,3},{6,0},{7,1},{8,14},{9,15},{10,... | collective-permute-start | bytes 393224 | tf_op jit(solution)/shard_map/ppermute | solution.py:158
  96.0 11.8 %collective-permute-start.26 = (bf16[32,2048]{1,0:T(8,128)(2,1)S(1)}, bf16[32,2048]{1,0:T(8,128)(2,1)S(1)}, u32[]{:S(2)}, u32[]{:S(2)}) collective-permute-start(bf16[32,2048]{1,0:T(8,128)(2,1)S(1)} %get-tuple-element.82), channel_id=1, source_target_pairs={{0,2},{1,3},{2,0},{3,1},{4,6},{5,7},{6,4},{7,5},{8,10},{9,11},{10,... | collective-permute-start | bytes 393224 | tf_op jit(solution)/shard_map/ppermute | solution.py:158
  96.7 12.4 %collective-permute-start.25 = (bf16[32,2048]{1,0:T(8,128)(2,1)S(1)}, bf16[32,2048]{1,0:T(8,128)(2,1)S(1)}, u32[]{:S(2)}, u32[]{:S(2)}) collective-permute-start(bf16[32,2048]{1,0:T(8,128)(2,1)S(1)} %get-tuple-element.83), channel_id=1, source_target_pairs={{0,4},{1,5},{2,6},{3,7},{4,0},{5,1},{6,2},{7,3},{8,12},{9,13},{10,... | collective-permute-start | bytes 393224 | tf_op jit(solution)/shard_map/ppermute | solution.py:158
